TPU v7x, 128 devices: a whole 4x4x4 slice. The times are simulated.
128 devices in a mesh: dp: 16 (over z, x_hi, core), ctx: 8 (over x_lo, y).
Axes of the slice: x: 4 (x_hi: 2, x_lo: 2; x = x_hi * 2 + x_lo), y: 4, z: 4, core: 2. Of those that a mesh axis runs over, the one named last changes fastest.
Arguments:
- tokens: bfloat16 [16384, 2048], P(('dp', 'ctx')), may hold values from -6 to 6
- positions: int32 [16384], P(('dp', 'ctx')), may hold values from 0 to 1023, as said below
- attn_in: bfloat16 [2048, 2560], P(('dp', 'ctx')), may hold values from -0.125 to 0.125
- attn_out: bfloat16 [2048, 2048], P(('dp', 'ctx')), may hold values from -0.5 to 0.5
- attn_gain: bfloat16 [2048], P(('dp', 'ctx')), may hold values from 0.5 to 1.5
- mlp_in: bfloat16 [2048, 11264], P(('dp', 'ctx')), may hold values from -0.125 to 0.125
- mlp_down: bfloat16 [2048, 5632], P(('dp', 'ctx')), may hold values from -0.078125 to 0.078125
- mlp_gain: bfloat16 [2048], P(('dp', 'ctx')), may hold values from 0.5 to 1.5
- cotangent: bfloat16 [16384, 2048], P(('dp', 'ctx')), may hold values from -6 to 6
Outputs:
- activations: bfloat16 [16384, 2048], P(('dp', 'ctx'))
- input_grad: float32 [16384, 2048], P(('dp', 'ctx'))
- grad_attn_in: float32 [2048, 2560], P(('dp', 'ctx'))
- grad_attn_out: float32 [2048, 2048], P(('dp', 'ctx'))
- grad_attn_gain: float32 [2048], P(('dp', 'ctx'))
- grad_mlp_in: float32 [2048, 11264], P(('dp', 'ctx'))
- grad_mlp_down: float32 [2048, 5632], P(('dp', 'ctx'))
- grad_mlp_gain: float32 [2048], P(('dp', 'ctx'))
Inputs may be any that keep to these rules, and one draw needn't show every extreme that they name: Within each sequence positions rise by one from token to token and restart at 0 where a document begins; the first document of a sequence may continue one begun earlier. One document of every sequence begins within its first 128 tokens and ends within its last 128.
All inputs are finite; a program needn't handle non-finite values.
Results may differ from a plain program's by a relative error of at most 0.019.
Values may be sent and summed in bfloat16 or wider, within the bound.
A program may use at most 192 MiB of HBM per device.

v0:
```python
import jax
import jax.numpy as jnp
from jax import lax
from jax.experimental import pallas as pl
from jax.experimental.pallas import tpu as pltpu
from jax.sharding import PartitionSpec as P


D = 2048
HEADS = 32
KV_HEADS = 4
HEAD_DIM = 64
FF = 5632
REPEAT = HEADS // KV_HEADS
TP = 4
Q_COLS = D // TP
PROJ = Q_COLS + 2 * HEAD_DIM
HID = FF // TP

EPS = 1e-05
ROPE_BASE = 10000.0
NEG_FILL = -1e30

MESH = pl.DeviceIdType.MESH
BF16 = jnp.bfloat16
F32 = jnp.float32

SPLITS = ((PROJ, 384), (2 * HID, HID), (HID, 640))
OUT_SPLIT = 1024
VMEM_LIMIT = 60 << 20

NN = ((1,), (0,))
NT = ((1,), (1,))
TN = ((0,), (0,))


def place():
    dp, ctx = lax.axis_index("dp"), lax.axis_index("ctx")
    return (dp // 2) % 2, ctx // 4, ctx % 4, dp // 4, dp % 2


def device(xh, xl, y, z, c):
    return (z * 4 + xh * 2 + c, xl * 4 + y)


def along_y(d):
    def to(xh, xl, y, z, c):
        return xh, xl, (y + d) % 4, z, c

    return to


def along_x(d):
    def to(xh, xl, y, z, c):
        x = (xh * 2 + xl + d) % 4
        return x // 2, x % 2, y, z, c

    return to


def along_z(d):
    def to(xh, xl, y, z, c):
        return xh, xl, y, (z + d) % 4, c

    return to


def sibling(xh, xl, y, z, c):
    return xh, xl, y, z, 1 - c


def half_partner(xh, xl, y, z, c):
    return xh, 1 - xl, y, z, c


def crossed(xh, xl, y, z, c):
    return xh, xl, z, y, c


def say_hello(routes, cross=False):
    here = place()
    barrier = pltpu.get_barrier_semaphore()
    for back in routes:
        pl.semaphore_signal(barrier, inc=1, device_id=device(*back(*here)), device_id_type=MESH)
    if cross:

        @pl.when(here[2] != here[3])
        def _():
            pl.semaphore_signal(barrier, inc=1, device_id=device(*crossed(*here)), device_id_type=MESH)


def meet(routes, cross=False):
    here = place()
    barrier = pltpu.get_barrier_semaphore()
    if not cross:
        pl.semaphore_wait(barrier, len(routes))
        return
    away = here[2] != here[3]

    @pl.when(away)
    def _():
        pl.semaphore_wait(barrier, len(routes) + 1)

    @pl.when(jnp.logical_not(away))
    def _():
        pl.semaphore_wait(barrier, len(routes))


ALL_LINES = [along(d) for along in (along_y, along_x, along_z) for d in (1, 2, 3)] + [sibling]


class Copies:
    def __init__(self, send, recv):
        self.send, self.recv, self.count = send, recv, 0

    def __call__(self, src, dst, to):
        k, self.count = self.count, self.count + 1
        return pltpu.make_async_remote_copy(
            src_ref=src,
            dst_ref=dst,
            send_sem=self.send.at[k],
            recv_sem=self.recv.at[k],
            device_id=device(*to(*place())),
            device_id_type=MESH,
        )


def comm_call(kernel, name, ident, ins, outs, copies, locals_=0):
    return pl.pallas_call(
        kernel,
        out_shape=outs,
        in_specs=[pl.BlockSpec(memory_space=pl.ANY)] * len(ins),
        out_specs=[pl.BlockSpec(memory_space=pl.ANY)] * len(outs),
        scratch_shapes=[
            pltpu.SemaphoreType.DMA((copies,)),
            pltpu.SemaphoreType.DMA((copies,)),
            pltpu.SemaphoreType.DMA((max(locals_, 1),)),
        ],
        name=name,
        compiler_params=pltpu.CompilerParams(collective_id=ident, has_side_effects=True),
    )(*ins)


def struct(shape, dtype=BF16):
    return jax.ShapeDtypeStruct(shape, dtype)


class RingGather:
    def __init__(self, copy, own, dst, y):
        half = dst.shape[2] // 2
        lo, hi = pl.ds(0, half), pl.ds(half, half)
        back, on = (y + 3) % 4, (y + 1) % 4

        def first(cols, to):
            return copy(own.at[:, cols], dst.at[y, :, cols], to)

        def one(slot, cols, to):
            at = dst.at[slot, :, cols]
            return copy(at, at, to)

        self.first = [first(lo, along_y(1)), first(hi, along_y(3)), first(hi, along_y(1)), first(lo, along_y(3))]
        self.second = [one(back, lo, along_y(1)), one(on, hi, along_y(3))]

    def start(self):
        for cp in self.first:
            cp.start()

    def turn(self):
        for got, cp in zip(self.first, self.second):
            got.wait_recv()
            cp.start()

    def near(self):
        for cp in self.first[2:]:
            cp.wait_recv()

    def far(self):
        for cp in self.second:
            cp.wait_recv()

    def sent(self):
        for cp in self.first + self.second:
            cp.wait_send()


class RingSum:
    def __init__(self, copy, part, halves, whole, y):
        half = part.shape[2] // 2
        lo, hi = pl.ds(0, half), pl.ds(half, half)
        self.part, self.halves, self.whole, self.y = part, halves, whole, y
        self.cols = (lo, hi)
        far, on, back = (y + 2) % 4, (y + 1) % 4, (y + 3) % 4
        self.far = [
            copy(part.at[far, :, lo], halves.at[0], along_y(1)),
            copy(part.at[far, :, hi], halves.at[1], along_y(3)),
        ]
        self.near = [
            copy(part.at[on, :, hi], whole.at[0, :, hi], along_y(1)),
            copy(part.at[back, :, lo], whole.at[1, :, lo], along_y(3)),
        ]
        self.last = [
            copy(part.at[on, :, lo], whole.at[0, :, lo], along_y(1)),
            copy(part.at[back, :, hi], whole.at[1, :, hi], along_y(3)),
        ]
        self.slots = (on, back)

    def start(self):
        for cp in self.far + self.near:
            cp.start()

    def turn(self):
        for k in range(2):
            self.far[k].wait_recv()
            slot, cols = self.slots[k], self.cols[k]

            def body(r, _, slot=slot, cols=cols, k=k):
                rows = pl.ds(r * 32, 32)
                both = self.part[slot, rows, cols].astype(F32) + self.halves[k, rows].astype(F32)
                self.part[slot, rows, cols] = both.astype(BF16)
                return 0

            lax.fori_loop(0, self.part.shape[1] // 32, body, 0)
            self.last[k].start()

    def finish(self):
        for cp in self.near + self.last:
            cp.wait_recv()

    def rows(self, rows):
        own = self.part[self.y, rows].astype(F32)
        return own + self.whole[0, rows].astype(F32) + self.whole[1, rows].astype(F32)

    def sent(self):
        for cp in self.far + self.near + self.last:
            cp.wait_send()


class Gather:
    def __init__(self, copy, out, a, at, rows_only=False):
        xh, xl, y, z, c = at
        cols = out.shape[-1]
        left, right = pl.ds(0, a), pl.ds(a, cols - a)
        def cut(half, n):
            return slice(None) if half is None else pl.ds(half * (n // 2), n // 2)

        if rows_only:
            block = lambda z, x, c, cols: out.at[x[0], c, x[1], z, :, cols]
            z_line = lambda x, c, cols, half: out.at[x[0], c, x[1], cut(half, 4), :, cols]
            x_line = lambda z, c, cols, half: out.at[cut(half, 2), c, :, z, :, cols]
        else:
            block = lambda z, x, c, cols: out.at[z, x[0], c, pl.ds(x[1] * 64, 64), cols]
            z_line = lambda x, c, cols, half: out.at[cut(half, 4), x[0], c, pl.ds(x[1] * 64, 64), cols]
            x_line = lambda z, c, cols, half: out.at[z, cut(half, 2), c, :, cols]

        def same(ref, to):
            return copy(ref, ref, to)

        here = (xh, xl)
        self.first = []
        for d in (1, 3, 2):
            self.first.append(same(block(z, here, c, left), along_x(d)))
            self.first.append(same(block(z, here, c, right), along_z(d)))
        a_lo, a_hi = lambda z: x_line(z, c, left, 0), lambda z: x_line(z, c, left, 1)
        b_lo, b_hi = lambda x: z_line(x, c, right, 0), lambda x: z_line(x, c, right, 1)
        z_at = [(z + d) % 4 for d in range(4)]
        x_at = [along_x(d)(*at)[:2] for d in range(4)]
        self.lines = []
        for lo, hi, spots, along in ((a_lo, a_hi, z_at, along_z), (b_lo, b_hi, x_at, along_x)):
            going = [
                same(lo(spots[0]), along(1)),
                same(hi(spots[0]), along(3)),
                same(hi(spots[0]), along(1)),
                same(lo(spots[0]), along(3)),
            ]
            on = [same(lo(spots[3]), along(1)), same(hi(spots[1]), along(3))]
            self.lines.append((going, on))
        self.core = [same(block(z, here, c, pl.ds(0, cols)), sibling)]
        for d in (1, 3, 2):
            self.core.append(same(block(z, x_at[d], c, left), sibling))
            self.core.append(same(block(z_at[d], here, c, right), sibling))
        self.core_lines = []
        for d in (3, 1, 2):
            self.core_lines.append(
                (same(x_line(z_at[d], c, left, None), sibling), same(z_line(x_at[d], c, right, None), sibling))
            )

    def start(self):
        for cp in self.first:
            cp.start()
        self.core[0].start()

    def turn(self):
        for cp in self.first:
            cp.wait_recv()
        for going, _ in self.lines:
            for cp in going:
                cp.start()
        for cp in self.core[1:]:
            cp.start()

    def pass_on(self):
        for going, on in self.lines:
            for got, cp in zip(going[:2], on):
                got.wait_recv()
                cp.start()

    def near(self):
        for k, (going, _) in enumerate(self.lines):
            for side in range(2):
                going[2 + side].wait_recv()
                self.core_lines[side][k].start()

    def far(self):
        for k, (_, on) in enumerate(self.lines):
            for cp in on:
                cp.wait_recv()
            self.core_lines[2][k].start()

    def finish(self):
        for cp in self.core + [cp for pair in self.core_lines for cp in pair]:
            cp.wait_recv()

    def sent(self):
        for going, on in self.lines:
            for cp in going + on:
                cp.wait_send()
        for cp in self.first + self.core + [cp for pair in self.core_lines for cp in pair]:
            cp.wait_send()


def dot(left, right, dims=((1,), (0,))):
    return lax.dot_general(left, right, (dims, ((), ())), preferred_element_type=F32)


def swap_halves(v):
    lane = lax.broadcasted_iota(jnp.int32, v.shape, 1)
    return jnp.where(lane % 64 < 32, pltpu.roll(v, 96, 1), pltpu.roll(v, 32, 1))


def forward_attention(tokens, cotangent, spots, freqs, w_proj, w_gu, w_down, out_rows, ident):
    rows = tokens.shape[0]
    count = 4 * rows
    groups = [w_proj, w_gu, w_down]

    def kernel(
        tok_ref, cot_ref, spot_ref, freq_ref, wp, wg, wd, wo,
        normed_out, cot_all, gp, gg, gd, go, q_out, kv_out, att_out, lse_out, spot_out, middle_out, two_all,
        tok, normed, wp_v, wo_v, q_s, kv, vx, bias, att, part, halves, whole, spot_all, own_two, send, recv, local,
    ):
        say_hello(ALL_LINES, True)
        at = place()
        xh, xl, y, z, c = at
        copy = Copies(send, recv)
        slot = pl.ds(xl * 64 + y * 16, 16)
        nlocal = [0]

        def near(src, dst):
            cp = pltpu.make_async_copy(src, dst, local.at[nlocal[0]])
            nlocal[0] += 1
            return cp

        to_y = []
        stay = []
        for i, o in ((wp, gp), (wg, gg), (wd, gd)):
            to_y.append([copy(i.at[(y + d) % 4], o.at[z, xh, c, slot], along_y(d)) for d in (1, 3, 2)])
            stay.append(near(i.at[y], o.at[z, xh, c, slot]))
        over = copy(wo, go.at[xh, c, xl, y], crossed)
        keep = near(wo, go.at[xh, c, xl, z])
        spot_copies = [copy(spot_all.at[y], spot_all.at[y], along_y(d)) for d in (1, 3, 2)]
        tok_ring = RingGather(copy, tok_ref, tok, y)
        cot_ring = RingGather(copy, cot_ref, cot_all, y)
        two_ring = RingGather(copy, own_two, two_all, y)
        branch = RingSum(copy, part, halves, whole, y)
        kv_copy = copy(kv.at[1], kv.at[0], half_partner)
        g_proj = Gather(copy, gp, SPLITS[0][1], at)
        g_gu = Gather(copy, gg, SPLITS[1][1], at)
        g_down = Gather(copy, gd, SPLITS[2][1], at)
        g_out = Gather(copy, go, OUT_SPLIT, at, True)

        cot_own = near(cot_ref, cot_all.at[y])
        tok_own = near(tok_ref, tok.at[y])
        tok_own.start()
        cot_own.start()
        spot_all[y] = spot_ref[...]
        for cp in stay:
            cp.start()
        meet(ALL_LINES, True)
        away = y != z
        for cp in to_y[0]:
            cp.start()

        @pl.when(away)
        def _():
            over.start()

        @pl.when(jnp.logical_not(away))
        def _():
            keep.start()

        for cp in spot_copies + to_y[1] + to_y[2] + tok_ring.first:
            cp.start()

        def norm_block(k):
            def body(r, _):
                rs = pl.ds(r * 32, 32)
                v = tok[k, rs].astype(F32)
                inv = lax.rsqrt(jnp.mean(v * v, -1, keepdims=True) + EPS)
                normed[k, rs] = (v * inv).astype(BF16)
                return 0

            lax.fori_loop(0, rows // 32, body, 0)

        stay[0].wait()
        for cp in to_y[0]:
            cp.wait_recv()
        g_proj.start()

        @pl.when(away)
        def _():
            over.wait()

        @pl.when(jnp.logical_not(away))
        def _():
            keep.wait()

        g_out.start()
        tok_own.wait()
        norm_block(y)
        g_proj.turn()
        stay[1].wait()
        stay[2].wait()
        for cp in to_y[1] + to_y[2]:
            cp.wait_recv()
        g_gu.start()
        g_down.start()
        g_proj.pass_on()
        g_out.turn()
        for cp in spot_copies:
            cp.wait_recv()
        tok_ring.turn()
        g_proj.near()
        g_proj.far()

        cos, sin = [], []
        freq, sign = freq_ref[0:1, :], freq_ref[1:2, :]
        spot_cols = []
        for k in range(4):
            col = jnp.transpose(jnp.broadcast_to(spot_all[k, 0:1, :], (128, 128)))
            spot_out[k] = spot_all[k]
            spot_cols.append(col)
            cos.append(jnp.cos(col * freq))
            sin.append(jnp.sin(col * freq) * sign)
        cos, sin = jnp.concatenate(cos, 0), jnp.concatenate(sin, 0)
        low_half = xl == 0
        reach = jnp.where(low_half, -1.0, 2048.0)
        for k in range(4):
            for j in range(8):
                row = lax.broadcasted_iota(jnp.int32, (128, 128), 0) + k * 128
                col = lax.broadcasted_iota(jnp.int32, (128, 128), 1) + j * 128
                apart = (row - col + 512).astype(F32)
                seen = apart <= spot_cols[k]
                if j < 4:
                    seen = seen & (apart <= reach)
                else:
                    seen = seen & (col - 512 <= row)
                bias[pl.ds(k * 128, 128), pl.ds(j * 128, 128)] = jnp.where(seen, 0.0, NEG_FILL)

        g_proj.finish()
        wp_load = near(gp, wp_v)
        wp_load.start()
        g_out.pass_on()
        tok_ring.near()
        norm_block((y + 3) % 4)
        norm_block((y + 1) % 4)
        g_out.near()
        tok_ring.far()
        cot_ring.start()
        norm_block((y + 2) % 4)
        normed_save = near(normed, normed_out)
        normed_save.start()

        wp_load.wait()
        left = normed[...].reshape(count, D)
        lane = lax.broadcasted_iota(jnp.int32, (count, 128), 1)
        upper = lane >= 64
        raw = dot(left, wp_v[:, :, :, :, pl.ds(Q_COLS, 128)].reshape(D, 128))
        turned = raw * jnp.where(upper, 1.0, cos) + swap_halves(raw) * jnp.where(upper, 0.0, sin)
        kv[1] = turned.astype(BF16)
        kv_copy.start()
        g_out.far()
        g_gu.turn()
        g_down.turn()
        for j in range(2):
            raw2 = dot(left, wp_v[:, :, :, :, pl.ds(j * 256, 256)].reshape(D, 256))
            for e in range(2):
                raw = raw2[:, e * 128 : e * 128 + 128]
                turned = (raw * cos + swap_halves(raw) * sin).astype(BF16).astype(F32) * (HEAD_DIM ** (-0.5))
                pair = j * 2 + e
                q_s[2 * pair] = jnp.where(upper, 0.0, turned).astype(BF16)
                q_s[2 * pair + 1] = jnp.where(upper, 0.0, pltpu.roll(turned, 64, 1)).astype(BF16)
        kv_copy.wait_recv()
        for k in range(2):
            vx[k] = jnp.where(upper, kv[k].astype(F32), 1.0).astype(BF16)
        q_save = near(q_s, q_out)
        q_save.start()
        kv_save = near(kv, kv_out)
        kv_save.start()
        g_out.finish()
        wo_load = near(go, wo_v)
        wo_load.start()

        def attend(pair):
            for b in range(2):
                rs = pl.ds(b * 256, 256)
                seen = 256 * (b + 1)
                lane = lax.broadcasted_iota(jnp.int32, (256, 128), 1) < 64
                found = []
                for e in range(2):
                    q = q_s[2 * pair + e, rs]
                    s0 = dot(q, kv[0], NT) + bias[rs, pl.ds(0, 512)]
                    s1 = dot(q, kv[1, pl.ds(0, seen)], NT) + bias[rs, pl.ds(512, seen)]
                    m = jnp.maximum(jnp.max(s0, -1, keepdims=True), jnp.max(s1, -1, keepdims=True))
                    p0 = jnp.exp(s0 - m).astype(BF16)
                    p1 = jnp.exp(s1 - m).astype(BF16)
                    o = dot(p0, vx[0]) + dot(p1, vx[1, pl.ds(0, seen)])
                    r = pltpu.roll(o, 64, 1)
                    found.append((o, r))
                    log_total = m + jnp.log(jnp.where(lane, o, r))
                    lse_out[2 * pair + e, :, rs] = jnp.transpose(log_total)[0:8]
                (o, r), (o2, r2) = found
                both = jnp.where(lane, r / o, o2 / r2)
                att[rs, pl.ds(pl.multiple_of(pair * 128, 128), 128)] = both.astype(BF16)

        def two_pairs(k):
            def body(i, _):
                attend(2 * k + i)
                return 0

            lax.fori_loop(0, 2, body, 0)

        two_pairs(0)
        cot_ring.turn()
        two_pairs(1)
        att_save = near(att, att_out)
        att_save.start()
        wo_load.wait()

        for j in range(4):
            cols = pl.ds(j * 512, 512)
            w = wo_v[:, :, :, :, :, cols].reshape(Q_COLS, 512)
            part[:, :, cols] = dot(att[...], w).astype(BF16).reshape(4, rows, 512)
        branch.start()
        g_gu.pass_on()
        g_down.pass_on()
        branch.turn()
        g_gu.near()
        g_down.near()
        cot_ring.near()
        cot_ring.far()
        branch.finish()

        def mid(r, _):
            rs = pl.ds(r * 32, 32)
            v = tok_ref[rs].astype(F32) + branch.rows(rs)
            middle_out[rs] = v
            inv = lax.rsqrt(jnp.mean(v * v, -1, keepdims=True) + EPS)
            own_two[rs] = (v * inv).astype(BF16)
            return 0

        lax.fori_loop(0, rows // 32, mid, 0)
        two_own = near(own_two, two_all.at[y])
        two_own.start()
        two_ring.start()
        two_ring.turn()
        g_gu.far()
        g_down.far()
        two_ring.near()
        two_ring.far()
        g_gu.finish()
        g_down.finish()
        for cp in (cot_own, normed_save, q_save, kv_save, att_save, two_own):
            cp.wait()
        for group in to_y:
            for cp in group:
                cp.wait_send()
        for cp in spot_copies + [kv_copy]:
            cp.wait_send()
        for thing in (g_proj, g_out, g_gu, g_down, tok_ring, cot_ring, two_ring, branch):
            thing.sent()

    anywhere, vmem = pl.BlockSpec(memory_space=pl.ANY), pl.BlockSpec(memory_space=pltpu.VMEM)
    outs = [
        (struct((4, rows, D)), anywhere),
        (struct((4, rows, D)), anywhere),
        (struct((4, 2, 2, 128, PROJ)), anywhere),
        (struct((4, 2, 2, 128, 2 * HID)), anywhere),
        (struct((4, 2, 2, 128, HID)), anywhere),
        (struct((2, 2, 2, 4, 16, D)), anywhere),
        (struct((REPEAT, count, 128)), anywhere),
        (struct((2, count, 128)), anywhere),
        (struct((count, Q_COLS)), anywhere),
        (struct((REPEAT, 8, count), F32), vmem),
        (struct((4, 8, 128), F32), vmem),
        (struct((rows, D), F32), vmem),
        (struct((4, rows, D)), anywhere),
    ]
    copies = 9 + 1 + 3 + 6 * 3 + 6 + 1 + 31 * 4
    return pl.pallas_call(
        kernel,
        out_shape=[o[0] for o in outs],
        in_specs=[vmem] * 8,
        out_specs=[o[1] for o in outs],
        scratch_shapes=[
            pltpu.VMEM((4, rows, D), BF16),
            pltpu.VMEM((4, rows, D), BF16),
            pltpu.VMEM((4, 2, 2, 128, PROJ), BF16),
            pltpu.VMEM((2, 2, 2, 4, 16, D), BF16),
            pltpu.VMEM((REPEAT, count, 128), BF16),
            pltpu.VMEM((2, count, 128), BF16),
            pltpu.VMEM((2, count, 128), BF16),
            pltpu.VMEM((count, 2 * count), F32),
            pltpu.VMEM((count, Q_COLS), BF16),
            pltpu.VMEM((4, rows, D), BF16),
            pltpu.VMEM((2, rows, D // 2), BF16),
            pltpu.VMEM((2, rows, D), BF16),
            pltpu.VMEM((4, 8, 128), F32),
            pltpu.VMEM((rows, D), BF16),
            pltpu.SemaphoreType.DMA((copies,)),
            pltpu.SemaphoreType.DMA((copies,)),
            pltpu.SemaphoreType.DMA((16,)),
        ],
        name="forward_attention",
        compiler_params=pltpu.CompilerParams(
            collective_id=ident, has_side_effects=True, vmem_limit_bytes=VMEM_LIMIT
        ),
    )(tokens, cotangent, spots, freqs, w_proj, w_gu, w_down, out_rows)


def tiles(ref):
    if len(ref.shape) == 2:
        return [ref]
    return [t for k in range(ref.shape[0]) for t in tiles(ref.at[k])]


def add_up(dst, *others):
    for out, *terms in zip(tiles(dst), *[tiles(o) for o in others]):
        rows = out.shape[0]
        step = min(rows, 32)

        def body(r, _, out=out, terms=terms, step=step):
            rs = pl.ds(r * step, step)
            value = out[rs].astype(F32)
            for t in terms:
                value = value + t[rs].astype(F32)
            out[rs] = value.astype(BF16)
            return 0

        lax.fori_loop(0, rows // step, body, 0)


class LineSum:
    def __init__(self, copy, lo, hi, along, far, near):
        self.lo, self.hi, self.far_in, self.near_in = lo, hi, far, near
        self.far = [copy(lo(2), far.at[0], along(1)), copy(hi(2), far.at[1], along(3))]
        self.near = [copy(hi(1), near.at[0, 1], along(1)), copy(lo(3), near.at[1, 0], along(3))]
        self.last = [copy(lo(1), near.at[0, 0], along(1)), copy(hi(3), near.at[1, 1], along(3))]

    def start(self):
        for cp in self.far + self.near:
            cp.start()

    def turn(self):
        self.far[0].wait_recv()
        add_up(self.lo(1), self.far_in.at[0])
        self.last[0].start()
        self.far[1].wait_recv()
        add_up(self.hi(3), self.far_in.at[1])
        self.last[1].start()

    def finish(self):
        for cp in self.near + self.last:
            cp.wait_recv()
        add_up(self.lo(0), self.near_in.at[0, 0], self.near_in.at[1, 0])
        add_up(self.hi(0), self.near_in.at[0, 1], self.near_in.at[1, 1])

    def sent(self):
        for cp in self.far + self.near + self.last:
            cp.wait_send()


class GradLines:
    def __init__(self, copy, terms, a, at, buffers, rows_only=False):
        xh, xl, y, z, c = at
        far_a, near_a, far_b, near_b = buffers
        cols = terms.shape[-1]
        left, right = pl.ds(0, a), pl.ds(a, cols - a)
        x_at = [along_x(d)(*at)[:2] for d in range(4)]
        z_at = [(z + d) % 4 for d in range(4)]
        if rows_only:
            spot = lambda x, z, cols: terms.at[x[0], c, x[1], z, :, cols]
            a_half = lambda h: lambda d: terms.at[h, c, :, z_at[d], :, left]
            b_half = lambda h: lambda d: terms.at[x_at[d][0], c, x_at[d][1], pl.ds(2 * h, 2), :, right]
        else:
            base = (lambda z, xh: (z, xh, c)) if len(terms.shape) == 5 else (lambda z, xh: (z, xh))
            spot = lambda x, z, cols: terms.at[base(z, x[0]) + (pl.ds(x[1] * 64, 64), cols)]
            a_half = lambda h: lambda d: terms.at[base(z_at[d], h) + (slice(None), left)]
            b_half = lambda h: lambda d: terms.at[
                base(pl.ds(2 * h, 2), x_at[d][0]) + (pl.ds(x_at[d][1] * 64, 64), right)
            ]
        self.lines = [
            LineSum(copy, a_half(0), a_half(1), along_z, far_a, near_a),
            LineSum(copy, b_half(0), b_half(1), along_x, far_b, near_b),
        ]
        self.spot_a = lambda x: spot(x, z, left)
        self.spot_b = lambda z: spot(x_at[0], z, right)

    def start(self):
        for line in self.lines:
            line.start()

    def turn(self):
        for line in self.lines:
            line.turn()

    def finish(self):
        for line in self.lines:
            line.finish()

    def sent(self):
        for line in self.lines:
            line.sent()


class GradOwners:
    def __init__(self, copy, local_copy, spot_a, spot_b, out, at, buffers, rows_only=False):
        xh, xl, y, z, c = at
        self.at, self.rows_only = at, rows_only
        got_a, got_b, own = buffers
        a, cols = got_a.shape[-1], own.shape[-1]
        self.second = []
        for d in (1, 3, 2):
            self.second.append(copy(spot_a(along_x(d)(*at)[:2]), got_a.at[d - 1], along_x(d)))
            self.second.append(copy(spot_b((z + d) % 4), got_b.at[d - 1], along_z(d)))
        self.mine = (spot_a((xh, xl)), spot_b(z))
        self.got = (got_a, got_b)
        self.own, self.cuts = own, (pl.ds(0, a), pl.ds(a, cols - a))
        if rows_only:
            self.over = copy(own, out, crossed)
            self.keep = local_copy(own, out)
        else:
            self.to_y = [copy(own.at[(y + d) % 4], out.at[y], along_y(d)) for d in (1, 3, 2)]
            self.keep = local_copy(own.at[y], out.at[y])

    def start(self):
        for cp in self.second:
            cp.start()

    def deliver(self):
        for cp in self.second:
            cp.wait_recv()
        for mine, got, cut in zip(self.mine, self.got, self.cuts):
            value = mine[...].astype(F32)
            for d in range(3):
                value = value + got[d].astype(F32)
            own = self.own
            if self.rows_only:
                own[:, cut] = value.astype(BF16)
            else:
                own[:, :, cut] = value.astype(BF16).reshape(4, 16, value.shape[-1])
        if self.rows_only:
            y, z = self.at[2], self.at[3]

            @pl.when(y != z)
            def _():
                self.over.start()

            @pl.when(y == z)
            def _():
                self.keep.start()

        else:
            for cp in self.to_y:
                cp.start()
            self.keep.start()

    def finish(self):
        if self.rows_only:
            y, z = self.at[2], self.at[3]

            @pl.when(y != z)
            def _():
                self.over.wait()

            @pl.when(y == z)
            def _():
                self.keep.wait()

        else:
            for cp in self.to_y:
                cp.wait()
            self.keep.wait()
        for cp in self.second:
            cp.wait_send()


def line_buffers(cols, a, rows_only=False):
    b = cols - a
    a_half, b_half = ((2, 16), (2, 16)) if rows_only else ((128,), (2, 64))
    return [
        pltpu.VMEM((2,) + a_half + (a,), BF16),
        pltpu.VMEM((2, 2) + a_half + (a,), BF16),
        pltpu.VMEM((2,) + b_half + (b,), BF16),
        pltpu.VMEM((2, 2) + b_half + (b,), BF16),
    ]


def owner_buffers(cols, a, rows_only=False):
    spot, own = (16, (16, cols)) if rows_only else (64, (4, 16, cols))
    return [pltpu.VMEM((3, spot, a), BF16), pltpu.VMEM((3, spot, cols - a), BF16), pltpu.VMEM(own, BF16)]


def rotation(spot_rows, freq_ref):
    cos, sin = [], []
    for k in range(4):
        col = jnp.transpose(jnp.broadcast_to(spot_rows[k, 0:1, :], (128, 128)))
        cos.append(jnp.cos(col * freq_ref[0:1, :]))
        sin.append(jnp.sin(col * freq_ref[0:1, :]) * freq_ref[1:2, :])
    return jnp.concatenate(cos, 0), jnp.concatenate(sin, 0)


def backward_attention(
    gu_a, gu_b, sum_down, out_part, branch_all, grad_middle, middle, tokens, freqs,
    spots, q_all, kv_all, attended, lse, normed_all, proj_w, out_w, ident,
):
    rows = tokens.shape[0]
    count = 4 * rows
    scale = HEAD_DIM ** (-0.5)

    def kernel(
        gu_a_ref, gu_b_ref, s_down, op_ref, br_ref, gm_ref, mid_ref, tok_ref, freq_ref,
        spot_ref, q_ref, kv_ref, att_ref, lse_ref, nm_ref, wp_ref, wo_ref,
        out_ref, ig_ref, o_proj, o_gu, o_down, o_out,
        v_gu_a, v_gu_b, v_down, part, halves, whole, halves2, whole2, br, q_s, do_s, kv, kvt, att, delta, bias, cos_s, sin_s,
        dkv, kv_send, kv_in, gp, normed, wp, wo, t_proj, rc_proj, t_out, rc_out, *rest,
    ):
        bufs, (send, recv, local) = rest[:24], rest[24:]
        say_hello(ALL_LINES, True)
        at = place()
        xh, xl, y, z, c = at
        copy = Copies(send, recv)
        nlocal = [0]

        def near(src, dst):
            cp = pltpu.make_async_copy(src, dst, local.at[nlocal[0]])
            nlocal[0] += 1
            return cp

        load_gu, load_gu_b, load_down = near(gu_a_ref, v_gu_a), near(gu_b_ref, v_gu_b), near(s_down, v_down)
        load_op, load_br, load_wo = near(op_ref, part), near(br_ref, br), near(wo_ref, wo)
        load_att, load_q = near(att_ref, att), near(q_ref, q_s)
        load_kv = near(kv_ref, kv)
        load_nm, load_wp = near(nm_ref, normed), near(wp_ref, wp)
        for cp in (load_br, load_wo, load_gu, load_gu_b, load_op, load_down, load_att, load_q, load_kv, load_nm, load_wp):
            cp.start()
        outs = RingSum(copy, part, halves, whole, y)
        ones = RingSum(copy, part, halves2, whole2, y)
        kv_copy = copy(kv_send, kv_in, half_partner)
        core_proj = copy(t_proj.at[:, :, 1 - c], rc_proj, sibling)
        core_out = copy(t_out.at[:, 1 - c], rc_out, sibling)
        gu_owners = GradOwners(
            copy,
            near,
            lambda x: v_gu_a.at[x[0], pl.ds(x[1] * 64, 64)],
            lambda z: v_gu_b.at[z],
            o_gu,
            at,
            bufs[0:3],
        )
        down_lines = GradLines(copy, v_down, SPLITS[2][1], at, bufs[3:7])
        down_owners = GradOwners(copy, near, down_lines.spot_a, down_lines.spot_b, o_down, at, bufs[7:10])
        proj_lines = GradLines(copy, t_proj, SPLITS[0][1], at, bufs[10:14])
        proj_owners = GradOwners(copy, near, proj_lines.spot_a, proj_lines.spot_b, o_proj, at, bufs[14:17])
        out_lines = GradLines(copy, t_out, OUT_SPLIT, at, bufs[17:21], True)
        out_owners = GradOwners(copy, near, out_lines.spot_a, out_lines.spot_b, o_out, at, bufs[21:24], True)

        cos, sin = rotation(spot_ref, freq_ref)
        cos_s[...] = cos
        sin_s[...] = sin
        reach = jnp.where(xl == 0, -1.0, 2048.0)
        for k in range(4):
            spots_row = spot_ref[k, 0:1, :]
            for j in range(8):
                key = lax.broadcasted_iota(jnp.int32, (128, 128), 0) + j * 128
                row = lax.broadcasted_iota(jnp.int32, (128, 128), 1) + k * 128
                apart = (row - key + 512).astype(F32)
                seen = apart <= spots_row
                if j < 4:
                    seen = seen & (apart <= reach)
                else:
                    seen = seen & (key - 512 <= row)
                bias[pl.ds(j * 128, 128), pl.ds(k * 128, 128)] = jnp.where(seen, 0.0, NEG_FILL)
        dkv[...] = jnp.zeros_like(dkv)

        meet(ALL_LINES, True)
        load_op.wait()
        outs.start()
        load_gu.wait()
        load_gu_b.wait()
        gu_owners.start()
        load_down.wait()
        down_lines.start()

        load_br.wait()
        load_wo.wait()
        load_att.wait()
        lane = lax.broadcasted_iota(jnp.int32, (count, 128), 1)
        for p in range(4):
            w = wo[p // 2, p % 2].reshape(128, D)
            low = dot(br[...].reshape(count, D), w, NT).astype(BF16).astype(F32)
            do_s[2 * p] = jnp.where(lane < 64, 0.0, pltpu.roll(low, 64, 1)).astype(BF16)
            do_s[2 * p + 1] = jnp.where(lane < 64, 0.0, low).astype(BF16)
            prod = jnp.transpose(low * att[:, pl.ds(p * 128, 128)].astype(F32))
            for e in range(2):
                total_row = jnp.sum(prod[e * 64 : e * 64 + 64], 0, keepdims=True)
                delta[2 * p + e] = jnp.broadcast_to(total_row, (8, count))
        outs.turn()

        for k in range(4):
            term = dot(att[:, pl.ds(k * 128, 128)], br[...].reshape(count, D), TN)
            t_out[k // 2, k % 2] = term.astype(BF16).reshape(2, 4, 16, D)
        core_out.start()
        load_q.wait()
        load_kv.wait()
        for k in range(2):
            turned = jnp.transpose(kv[pl.ds(k * count, count)].astype(F32)).astype(BF16)
            kvt[:, pl.ds(k * count, count)] = turned

        def backward(pair):
            for b in range(2):
                rs = pl.ds(b * 256, 256)
                seen = pl.ds(0, 512 + 256 * (b + 1))
                found = []
                for e in range(2):
                    h = 2 * pair + e
                    q, do = q_s[h, rs], do_s[h, rs]
                    st = dot(kv[seen], q, NT) + bias[seen, rs] - lse_ref[h, 0:1, rs]
                    p = jnp.exp(st)
                    dp = dot(kv[seen], do, NT)
                    ds = (p * (dp - delta[h, 0:1, rs])).astype(BF16)
                    dkv[seen] += dot(ds, q) + dot(p.astype(BF16), do)
                    found.append(dot(kvt[:, seen], ds)[0:64])
                both = jnp.transpose(jnp.concatenate(found, 0)) * scale
                both = both * cos_s[rs] - swap_halves(both) * sin_s[rs]
                gp[rs, pl.ds(pl.multiple_of(pair * 128, 128), 128)] = both.astype(BF16)

        def two_pairs(k):
            def body(i, _):
                backward(2 * k + i)
                return 0

            lax.fori_loop(0, 2, body, 0)

        two_pairs(0)
        down_lines.turn()
        gu_owners.deliver()
        two_pairs(1)
        kv_send[...] = dkv[pl.ds(0, count)].astype(BF16)
        kv_copy.start()
        core_out.wait_recv()
        add_up(t_out.at[:, c], rc_out)
        out_lines.start()
        down_lines.finish()
        down_owners.start()
        outs.finish()

        def finish_out(r, _):
            rs = pl.ds(r * 32, 32)
            out_ref[rs] = (mid_ref[rs] + outs.rows(rs)).astype(BF16)
            return 0

        lax.fori_loop(0, rows // 32, finish_out, 0)
        outs.sent()
        kv_copy.wait_recv()
        got = dkv[pl.ds(count, count)] + kv_in[...].astype(F32)
        back = got * cos_s[...] - swap_halves(got) * sin_s[...]
        gp[:, pl.ds(Q_COLS, 128)] = jnp.where(lane < 64, back, got).astype(BF16)

        load_wp.wait()
        for j in range(4):
            w = wp[j].reshape(512, PROJ)
            part[:, :, pl.ds(j * 512, 512)] = dot(gp[...], w, NT).astype(BF16).reshape(4, rows, 512)
        ones.start()
        load_nm.wait()
        for k in range(4):
            left = normed[:, :, pl.ds(k * 512, 512)].reshape(count, 512)
            t_proj[k] = dot(left, gp[...], TN).astype(BF16).reshape(2, 2, 128, PROJ)
        core_proj.start()
        out_lines.turn()
        ones.turn()
        down_owners.deliver()
        core_proj.wait_recv()
        for k in range(4):
            add_up(t_proj.at[k, :, c], rc_proj.at[k])
        proj_lines.start()
        out_lines.finish()
        out_owners.start()
        proj_lines.turn()
        ones.finish()

        def finish_in(r, _):
            rs = pl.ds(r * 32, 32)
            v = tok_ref[rs].astype(F32)
            inv = lax.rsqrt(jnp.mean(v * v, -1, keepdims=True) + EPS)
            v = v * inv
            g = ones.rows(rs)
            ig_ref[rs] = gm_ref[rs] + inv * (g - v * jnp.mean(g * v, -1, keepdims=True))
            return 0

        lax.fori_loop(0, rows // 32, finish_in, 0)
        proj_lines.finish()
        proj_owners.start()
        out_owners.deliver()
        proj_owners.deliver()
        ones.sent()
        for cp in (kv_copy, core_proj, core_out):
            cp.wait_send()
        for owners in (gu_owners, down_owners, out_owners, proj_owners):
            owners.finish()
        for lines in (down_lines, out_lines, proj_lines):
            lines.sent()

    anywhere, vmem = pl.BlockSpec(memory_space=pl.ANY), pl.BlockSpec(memory_space=pltpu.VMEM)
    in_specs = [anywhere] * 5 + [vmem] * 5 + [anywhere] * 3 + [vmem] + [anywhere] * 3
    outs = [
        (struct((rows, D)), vmem),
        (struct((rows, D), F32), vmem),
        (struct((4, 16, PROJ)), anywhere),
        (struct((4, 16, 2 * HID)), anywhere),
        (struct((4, 16, HID)), anywhere),
        (struct((16, D)), anywhere),
    ]
    whole = lambda: [pltpu.VMEM((2, rows, D // 2), BF16), pltpu.VMEM((2, rows, D), BF16)]
    copies = 12 + 3 + 9 + 21 * 2 + 19
    return pl.pallas_call(
        kernel,
        out_shape=[o[0] for o in outs],
        in_specs=in_specs,
        out_specs=[o[1] for o in outs],
        scratch_shapes=[
            pltpu.VMEM((2, 128, SPLITS[1][1]), BF16),
            pltpu.VMEM((4, 64, 2 * HID - SPLITS[1][1]), BF16),
            pltpu.VMEM((4, 2, 128, HID), BF16),
            pltpu.VMEM((4, rows, D), BF16),
            *whole(),
            *whole(),
            pltpu.VMEM((4, rows, D), BF16),
            pltpu.VMEM((REPEAT, count, 128), BF16),
            pltpu.VMEM((REPEAT, count, 128), BF16),
            pltpu.VMEM((2 * count, 128), BF16),
            pltpu.VMEM((128, 2 * count), BF16),
            pltpu.VMEM((count, Q_COLS), BF16),
            pltpu.VMEM((REPEAT, 8, count), F32),
            pltpu.VMEM((2 * count, count), F32),
            pltpu.VMEM((count, 128), F32),
            pltpu.VMEM((count, 128), F32),
            pltpu.VMEM((2 * count, 128), F32),
            pltpu.VMEM((count, 128), BF16),
            pltpu.VMEM((count, 128), BF16),
            pltpu.VMEM((count, PROJ), BF16),
            pltpu.VMEM((4, rows, D), BF16),
            pltpu.VMEM((4, 2, 2, 128, PROJ), BF16),
            pltpu.VMEM((2, 2, 2, 4, 16, D), BF16),
            pltpu.VMEM((4, 2, 2, 128, PROJ), BF16),
            pltpu.VMEM((4, 2, 128, PROJ), BF16),
            pltpu.VMEM((2, 2, 2, 4, 16, D), BF16),
            pltpu.VMEM((2, 2, 4, 16, D), BF16),
            *owner_buffers(2 * HID, SPLITS[1][1]),
            *line_buffers(HID, SPLITS[2][1]),
            *owner_buffers(HID, SPLITS[2][1]),
            *line_buffers(PROJ, SPLITS[0][1]),
            *owner_buffers(PROJ, SPLITS[0][1]),
            *line_buffers(D, OUT_SPLIT, True),
            *owner_buffers(D, OUT_SPLIT, True),
            pltpu.SemaphoreType.DMA((copies,)),
            pltpu.SemaphoreType.DMA((copies,)),
            pltpu.SemaphoreType.DMA((16,)),
        ],
        name="backward_attention",
        compiler_params=pltpu.CompilerParams(
            collective_id=ident, has_side_effects=True, vmem_limit_bytes=VMEM_LIMIT
        ),
    )(
        gu_a, gu_b, sum_down, out_part, branch_all, grad_middle, middle, tokens, freqs,
        spots, q_all, kv_all, attended, lse, normed_all, proj_w, out_w,
    )


def feed_forward(seq_two, seq_cot, gu_w, down_w, middle, cotangent, ident):
    rows = middle.shape[0]
    count = 4 * rows
    tiles_gu, pairs = HID // 128, HID // 256

    def kernel(
        two_ref, cot_ref, wg_ref, wd_ref, mid_ref, own_cot,
        branch_all, gm_ref, gu_a, gu_b, s_down, op_out,
        part, halves, whole, two, gu, cot, hid, gh, turned, t_gu, t_down, rc_gu, rc_down, branch, op,
        far_a, near_a, far_b, near_b, send, recv, local, weights,
    ):
        partners = [along_y(1), along_y(3), along_x(1), along_x(3), along_z(1), along_z(3), sibling]
        say_hello(partners)
        at = place()
        xh, xl, y, z, c = at
        copy = Copies(send, recv)
        nlocal = [0]

        def near(src, dst):
            cp = pltpu.make_async_copy(src, dst, local.at[nlocal[0]])
            nlocal[0] += 1
            return cp

        def load_gu(j):
            tile = pl.ds(pl.multiple_of(j * 256, 256), 256)
            return pltpu.make_async_copy(wg_ref.at[:, :, :, :, tile], t_gu.at[:, :, :, :, tile], weights.at[j])

        def load_down(j, width=256):
            tile = pl.ds(pl.multiple_of(j * 256, 256), width)
            return pltpu.make_async_copy(
                wd_ref.at[:, :, :, :, tile], t_down.at[:, :, :, :, tile], weights.at[tiles_gu + j]
            )

        load_cot, load_two = near(cot_ref, cot), near(two_ref, two)
        load_cot.start()
        last_down = load_down(pairs, HID - 256 * pairs)

        def begin_down(j, _):
            load_down(j).start()
            return 0

        def begin_gu(j, _):
            load_gu(j).start()
            return 0

        lax.fori_loop(0, pairs, begin_down, 0)
        last_down.start()
        load_two.start()
        lax.fori_loop(0, tiles_gu, begin_gu, 0)
        ring = RingSum(copy, part, halves, whole, y)
        gather = RingGather(copy, branch, branch_all, y)
        own = near(branch, branch_all.at[y])
        cores = [
            (copy(t_gu.at[k, :, 1 - c], rc_gu.at[k], sibling), copy(t_down.at[k, :, 1 - c], rc_down.at[k], sibling))
            for k in range(4)
        ]
        saves = [near(t_down.at[k, :, c], s_down.at[k]) for k in range(4)]
        lines = GradLines(copy, t_gu, SPLITS[1][1], at, (far_a, near_a, far_b, near_b))
        saves_gu = [
            near(t_gu.at[z, :, c, :, pl.ds(0, HID)], gu_a),
            near(t_gu.at[:, xh, c, pl.ds(xl * 64, 64), pl.ds(HID, HID)], gu_b),
        ]
        save_op = near(op, op_out)
        load_cot.wait()

        def hidden_back(j, _):
            load_down(j).wait()
            tile = pl.ds(pl.multiple_of(j * 256, 256), 256)
            gh[:, tile] = dot(cot[...].reshape(count, D), t_down[:, :, :, :, tile].reshape(D, 256))
            return 0

        lax.fori_loop(0, pairs, hidden_back, 0)
        last_down.wait()
        tile = pl.ds(256 * pairs, HID - 256 * pairs)
        gh[:, tile] = dot(cot[...].reshape(count, D), t_down[:, :, :, :, tile].reshape(D, HID - 256 * pairs))
        load_two.wait()

        def hidden(j, _):
            load_gu(j).wait()
            both = pl.ds(pl.multiple_of(j * 256, 256), 256)
            one = pl.ds(pl.multiple_of(j * 128, 128), 128)
            gate_up = dot(two[...].reshape(count, D), t_gu[:, :, :, :, both].reshape(D, 256))
            gate, up = gate_up[:, :128], gate_up[:, 128:]
            back = gh[:, one]
            sigmoid = jax.nn.sigmoid(gate)
            silu = gate * sigmoid
            hid[:, one] = (silu * up).astype(BF16)
            grad_gate = back * up * sigmoid * (1.0 + gate * (1.0 - sigmoid))
            gu[:, both] = jnp.concatenate([grad_gate, back * silu], 1).astype(BF16)
            return 0

        lax.fori_loop(0, tiles_gu, hidden, 0)

        def part_two(k, _):
            cols = pl.ds(pl.multiple_of(k * 512, 512), 512)
            part[:, :, cols] = dot(gu[...], t_gu[k].reshape(512, 2 * HID), NT).astype(BF16).reshape(4, rows, 512)
            return 0

        lax.fori_loop(0, 4, part_two, 0)
        meet(partners)
        ring.start()

        def part_out(k, _):
            cols = pl.ds(pl.multiple_of(k * 512, 512), 512)
            op[:, :, cols] = dot(hid[...], t_down[k].reshape(512, HID), NT).astype(BF16).reshape(4, rows, 512)
            return 0

        def terms_gu(k):
            cols = pl.ds(k * 512, 512)
            turned[...] = jnp.transpose(two[:, :, cols].reshape(count, 512))

            def some(j, _):
                tile = pl.ds(pl.multiple_of(j * 256, 256), 256)
                t_gu[k, :, :, :, tile] = dot(turned[...], gu[:, tile]).astype(BF16).reshape(2, 2, 128, 256)
                return 0

            lax.fori_loop(0, 2 * HID // 256, some, 0)
            cores[k][0].start()

        def terms_down(k):
            cols = pl.ds(k * 512, 512)
            turned[...] = jnp.transpose(cot[:, :, cols].reshape(count, 512))

            def more(j, width=256):
                tile = pl.ds(pl.multiple_of(j * 256, 256), width)
                t_down[k, :, :, :, tile] = dot(turned[...], hid[:, tile]).astype(BF16).reshape(2, 2, 128, width)
                return 0

            lax.fori_loop(0, pairs, lambda j, _: more(j), 0)
            more(pairs, HID - 256 * pairs)
            cores[k][1].start()

        terms_gu(0)
        ring.turn()
        for k in (1, 2, 3):
            terms_gu(k)
        for k in range(4):
            cores[k][0].wait_recv()
            add_up(t_gu.at[k, :, c], rc_gu.at[k])
        lines.start()
        ring.finish()

        def back(r, _):
            rs = pl.ds(r * 32, 32)
            v = mid_ref[rs]
            inv = lax.rsqrt(jnp.mean(v * v, -1, keepdims=True) + EPS)
            v = v * inv
            g = ring.rows(rs)
            value = own_cot[rs].astype(F32) + inv * (g - v * jnp.mean(g * v, -1, keepdims=True))
            gm_ref[rs] = value
            branch[rs] = value.astype(BF16)
            return 0

        lax.fori_loop(0, rows // 32, back, 0)
        gather.start()
        own.start()
        lax.fori_loop(0, 4, part_out, 0)
        save_op.start()
        gather.turn()
        terms_down(0)
        lines.turn()
        for k in (1, 2, 3):
            terms_down(k)
        for k in range(4):
            cores[k][1].wait_recv()
            add_up(t_down.at[k, :, c], rc_down.at[k])
            saves[k].start()
        gather.near()
        gather.far()
        lines.finish()
        for cp in saves_gu:
            cp.start()
        own.wait()
        save_op.wait()
        for cp in saves + saves_gu:
            cp.wait()
        for pair in cores:
            for cp in pair:
                cp.wait_send()
        lines.sent()
        ring.sent()
        gather.sent()

    anywhere, vmem = pl.BlockSpec(memory_space=pl.ANY), pl.BlockSpec(memory_space=pltpu.VMEM)
    copies = 12 + 8 + 12
    return pl.pallas_call(
        kernel,
        out_shape=[
            struct((4, rows, D)),
            struct((rows, D), F32),
            struct((2, 128, HID)),
            struct((4, 64, HID)),
            struct((4, 2, 128, HID)),
            struct((4, rows, D)),
        ],
        in_specs=[anywhere] * 4 + [vmem] * 2,
        out_specs=[anywhere, vmem, anywhere, anywhere, anywhere, anywhere],
        scratch_shapes=[
            pltpu.VMEM((4, rows, D), BF16),
            pltpu.VMEM((2, rows, D // 2), BF16),
            pltpu.VMEM((2, rows, D), BF16),
            pltpu.VMEM((4, rows, D), BF16),
            pltpu.VMEM((count, 2 * HID), BF16),
            pltpu.VMEM((4, rows, D), BF16),
            pltpu.VMEM((count, HID), BF16),
            pltpu.VMEM((count, HID), F32),
            pltpu.VMEM((512, count), BF16),
            pltpu.VMEM((4, 2, 2, 128, 2 * HID), BF16),
            pltpu.VMEM((4, 2, 2, 128, HID), BF16),
            pltpu.VMEM((4, 2, 128, 2 * HID), BF16),
            pltpu.VMEM((4, 2, 128, HID), BF16),
            pltpu.VMEM((rows, D), BF16),
            pltpu.VMEM((4, rows, D), BF16),
            *line_buffers(2 * HID, SPLITS[1][1]),
            pltpu.SemaphoreType.DMA((copies,)),
            pltpu.SemaphoreType.DMA((copies,)),
            pltpu.SemaphoreType.DMA((14,)),
            pltpu.SemaphoreType.DMA((tiles_gu + pairs + 1,)),
        ],
        name="feed_forward",
        compiler_params=pltpu.CompilerParams(
            collective_id=ident, has_side_effects=True, vmem_limit_bytes=VMEM_LIMIT
        ),
    )(seq_two, seq_cot, gu_w, down_w, middle, cotangent)


def shards(tokens, positions, attn_in, attn_out, attn_gain, mlp_in, mlp_down, mlp_gain, cotangent):
    xh, xl, y, z, c = place()
    rows = tokens.shape[0]
    count = 4 * rows
    gain_one = attn_gain.astype(F32)[:, None]
    gain_two = mlp_gain.astype(F32)[:, None]

    in_f = attn_in.astype(F32)
    mlp_f = mlp_in.astype(F32)
    kv = HEAD_DIM * KV_HEADS
    by_y = lambda a: a.reshape(16, TP, -1)
    w_proj = jnp.concatenate(
        [by_y(in_f[:, :D]), by_y(in_f[:, D : D + kv]), by_y(in_f[:, D + kv :])], -1
    )
    w_proj = (w_proj * gain_one[:, :, None]).astype(BF16).transpose(1, 0, 2)
    by_tile = lambda a: a.reshape(16, TP, HID // 128, 1, 128)
    w_gu = jnp.concatenate([by_tile(mlp_f[:, :FF]), by_tile(mlp_f[:, FF:])], 3).reshape(16, TP, 2 * HID)
    w_gu = (w_gu * gain_two[:, :, None]).astype(BF16).transpose(1, 0, 2)
    w_down = by_y(mlp_down).transpose(1, 0, 2)
    spots = jnp.broadcast_to(positions.astype(F32)[None, :], (8, rows))
    lanes = jnp.arange(128)
    inv_freq = ROPE_BASE ** (-2.0 * (lanes % 32).astype(F32) / HEAD_DIM)
    signs = jnp.where(lanes % 64 < 32, -1.0, 1.0)
    freqs = jnp.zeros((8, 128), F32).at[0].set(inv_freq).at[1].set(signs)
    (normed_one_all, cot_all, proj_w, gu_w, down_w, out_w, q_all, kv_all, attended_low, lse, spots_all, middle, two_all) = (
        forward_attention(tokens, cotangent, spots, freqs, w_proj, w_gu, w_down, attn_out, 0)
    )
    branch_all, grad_middle, gu_a, gu_b, sum_down, out_part = feed_forward(
        two_all, cot_all, gu_w, down_w, middle, cotangent, 1
    )
    outputs, input_grad, own_proj, own_gu, own_down, own_out = backward_attention(
        gu_a, gu_b, sum_down, out_part, branch_all, grad_middle, middle, tokens, freqs,
        spots_all, q_all, kv_all.reshape(2 * count, 128), attended_low, lse, normed_one_all, proj_w, out_w, 2,
    )
    own_proj = own_proj.astype(F32).transpose(1, 0, 2)
    cut = lambda a, start, stop: a[:, :, start:stop].reshape(16, -1)
    own_proj = jnp.concatenate(
        [
            cut(own_proj, 0, Q_COLS),
            cut(own_proj, Q_COLS, Q_COLS + HEAD_DIM),
            cut(own_proj, Q_COLS + HEAD_DIM, PROJ),
        ],
        -1,
    )
    own_gu = own_gu.reshape(TP, 16, HID // 128, 2, 128).transpose(1, 3, 0, 2, 4).reshape(16, 2 * FF).astype(F32)
    own_down = own_down.astype(F32).transpose(1, 0, 2).reshape(16, FF)
    return (
        outputs,
        input_grad,
        own_proj * gain_one,
        own_out.astype(F32),
        jnp.sum(own_proj * in_f, -1),
        own_gu * gain_two,
        own_down,
        jnp.sum(own_gu * mlp_f, -1),
    )


def solution(mesh):
    both = ("dp", "ctx")
    wide, flat = P(both, None), P(both)
    in_specs = (wide, flat, wide, wide, flat, wide, wide, flat, wide)
    out_specs = (wide, wide, wide, wide, flat, wide, wide, flat)
    return jax.shard_map(shards, mesh=mesh, in_specs=in_specs, out_specs=out_specs, check_vma=False)
```

profile of v0, /device:TPU:0, one launch (start us, length us, event | category | flops | bytes accessed | tf_op | source)
XLA Modules:
  0.0 260.5 jit_solution(15638856022175264505)
XLA Ops:
  0.6 0.7 convert_element_type.49
  1.3 0.7 convert_element_type.52
  1.9 0.7 convert_element_type.46
  2.7 0.6 broadcast_in_dim.8.spot_ref
  3.3 0.7 fusion.8
  4.0 0.1 reshape.155
  4.1 0.1 reshape.156
  4.2 0.9 slice.61
  5.1 0.7 fusion.2.wp
  5.8 1.6 copy.38
  7.4 1.1 fusion.6
  8.5 0.1 reshape.157
  8.6 0.1 reshape.158
  8.7 0.6 copy.23
  9.3 0.6 reshape.159
  9.9 0.8 fusion.wg
  10.7 101.5 %forward_attention.1 = (bf16[4,128,2048]{2,1,0:T(8,128)(2,1)}, bf16[4,128,2048]{2,1,0:T(8,128)(2,1)}, bf16[4,2,2,128,640]{4,3,2,1,0:T(8,128)(2,1)}, bf16[4,2,2,1...) custom-call(bf16[128,2048]{1,0:T(8,128)(2,1)} %tok_ref.3, ...), custom_call_target="tpu_custom_call" | custom-call | tf_op jit(solution)/shard_map/forward_attention/pallas_call | solution.py:608
  112.3 72.0 %feed_forward.1 = (bf16[4,128,2048]{2,1,0:T(8,128)(2,1)}, f32[128,2048]{1,0:T(8,128)}, bf16[2,128,1408]{2,1,0:T(8,128)(2,1)}, bf16[4,64,1408]{2,1,0:T(8,128)(2,1...) custom-call(bf16[4,128,2048]{2,1,0:T(8,128)(2,1)} %get-tuple-element.57.two_ref, ...), custom_call_target="tpu_custom_call" | custom-call | tf_op jit(solution)/shard_map/feed_forward/pallas_call | solution.py:1283
  184.2 66.4 %backward_attention.1 = (bf16[128,2048]{1,0:T(8,128)(2,1)}, f32[128,2048]{1,0:T(8,128)}, bf16[4,16,640]{2,1,0:T(8,128)(2,1)}, bf16[4,16,2816]{2,1,0:T(8,128)(2,1...) custom-call(bf16[2,128,1408]{2,1,0:T(8,128)(2,1)} %get-tuple-element.62.gu_a_ref, ...), custom_call_target="tpu_custom_call" | custom-call | tf_op jit(solution)/shard_map/backward_attention/pallas_call | solution.py:1044
  250.7 1.6 convert_element_type.54
  252.3 0.9 convert_bitcast_fusion.1
  253.3 0.1 reshape.164
  253.4 0.1 reshape.163
  253.6 1.4 multiply_reduce_fusion.1
  255.0 0.8 copy.33
  255.7 0.3 reshape.171
  256.1 0.1 copy.37
  256.2 0.1 reshape.167
  256.4 0.3 copy-done
  256.7 1.6 multiply_reduce_fusion
  258.3 0.8 copy.45
  259.1 1.0 copy.46
  (30 shorter events, 0.3 us)
Async XLA Ops:
  2.7 6.0 %copy-start.6 = (f32[8,128]{1,0:T(8,128)}, f32[8,128]{1,0:T(8,128)S(1)}, u32[]{:S(2)}) copy-start(f32[8,128]{1,0:T(8,128)S(1)} %scatter.9.freq_ref) | copy-start | bytes 12292
  184.2 69.3 %copy-start.2 = (bf16[16,2560]{1,0:T(8,128)(2,1)S(1)}, bf16[16,2560]{1,0:T(8,128)(2,1)}, u32[]{:S(2)}) copy-start(bf16[16,2560]{1,0:T(8,128)(2,1)} %param.15) | copy-start | bytes 245764
  250.7 4.2 %copy-start.5 = (bf16[4,16,1408]{2,1,0:T(8,128)(2,1)S(1)}, bf16[4,16,1408]{2,1,0:T(8,128)(2,1)}, u32[]{:S(2)}) copy-start(bf16[4,16,1408]{2,1,0:T(8,128)(2,1)} %get-tuple-element.81) | copy-start | bytes 540676
  250.7 5.0 %copy-start.4 = (bf16[4,16,2816]{2,1,0:T(8,128)(2,1)S(1)}, bf16[4,16,2816]{2,1,0:T(8,128)(2,1)}, u32[]{:S(2)}) copy-start(bf16[4,16,2816]{2,1,0:T(8,128)(2,1)} %get-tuple-element.80) | copy-start | bytes 1081348
  255.7 1.0 copy-start
  256.2 2.9 %copy-start.1 = (f32[128,2048]{1,0:T(8,128)S(1)}, f32[128,2048]{1,0:T(8,128)}, u32[]{:S(2)}) copy-start(f32[128,2048]{1,0:T(8,128)} %get-tuple-element.101) | copy-start | bytes 3145732
  256.7 1.6 copy-start.3
where the time goes:
time: 264 us; the launch traced here: 261 us
  Pallas kernels  240 us (91%)
  local copies, waits for them, and re-layouts  10.2 us (4%)
  other arithmetic  9.08 us (3%)
    pallas_call x1, Pallas kernels, forward_attention(): pl.pallas_call(kernel, out_shape=[o[0] for o in outs], in_specs=[vmem] *...  102 us
    pallas_call x1, Pallas kernels, feed_forward(): pl.pallas_call(kernel, out_shape=[struct((4, rows, D)), struct((rows, D),...  72 us
    pallas_call x1, Pallas kernels, backward_attention(): pl.pallas_call(kernel, out_shape=[o[0] for o in outs], in_specs=in_specs,...  66.4 us

commit v1 on v0

--- a/solution.py
+++ b/solution.py
@@ -1,5 +1,6 @@
 import jax
 import jax.numpy as jnp
+import numpy as np
 from jax import lax
 from jax.experimental import pallas as pl
 from jax.experimental.pallas import tpu as pltpu
@@ -25,7 +26,7 @@
 BF16 = jnp.bfloat16
 F32 = jnp.float32
 
-SPLITS = ((PROJ, 384), (2 * HID, HID), (HID, 640))
+SPLITS = ((PROJ, 384), (2 * HID, 13 * 128), (HID, 640))
 OUT_SPLIT = 1024
 VMEM_LIMIT = 60 << 20
 
@@ -289,14 +290,14 @@
             cp.start()
         self.core[0].start()
 
-    def turn(self):
-        for cp in self.first:
-            cp.wait_recv()
-        for going, _ in self.lines:
-            for cp in going:
+    def turn(self, *which):
+        for k in which or (0, 1):
+            for cp in self.first[k::2]:
+                cp.wait_recv()
+            for cp in self.lines[k][0]:
                 cp.start()
-        for cp in self.core[1:]:
-            cp.start()
+            for cp in self.core[1 + k :: 2]:
+                cp.start()
 
     def pass_on(self):
         for going, on in self.lines:
@@ -337,15 +338,14 @@
     return jnp.where(lane % 64 < 32, pltpu.roll(v, 96, 1), pltpu.roll(v, 32, 1))
 
 
-def forward_attention(tokens, cotangent, spots, freqs, w_proj, w_gu, w_down, out_rows, ident):
+def forward_attention(tokens, cotangent, positions, freqs, gains, attn_in, mlp_in, mlp_down, out_rows, ident):
     rows = tokens.shape[0]
     count = 4 * rows
-    groups = [w_proj, w_gu, w_down]
 
     def kernel(
-        tok_ref, cot_ref, spot_ref, freq_ref, wp, wg, wd, wo,
+        tok_ref, cot_ref, spot_ref, freq_ref, gain_ref, in_ref, mlp_ref, down_ref, wo,
         normed_out, cot_all, gp, gg, gd, go, q_out, kv_out, att_out, lse_out, spot_out, middle_out, two_all,
-        tok, normed, wp_v, wo_v, q_s, kv, vx, bias, att, part, halves, whole, spot_all, own_two, send, recv, local,
+        wp, wg, wd, tok, normed, wp_v, wo_v, q_s, kv, vx, bias, att, part, halves, whole, spot_all, own_two, send, recv, local,
     ):
         say_hello(ALL_LINES, True)
         at = place()
@@ -369,8 +369,9 @@
         spot_copies = [copy(spot_all.at[y], spot_all.at[y], along_y(d)) for d in (1, 3, 2)]
         tok_ring = RingGather(copy, tok_ref, tok, y)
         cot_ring = RingGather(copy, cot_ref, cot_all, y)
-        two_ring = RingGather(copy, own_two, two_all, y)
-        branch = RingSum(copy, part, halves, whole, y)
+        row_halves = [pl.ds(0, rows // 2), pl.ds(rows // 2, rows // 2)]
+        two_rings = [RingGather(copy, own_two.at[r], two_all.at[:, r], y) for r in row_halves]
+        branches = [RingSum(copy, part.at[:, r], halves.at[:, r], whole.at[:, r], y) for r in row_halves]
         kv_copy = copy(kv.at[1], kv.at[0], half_partner)
         g_proj = Gather(copy, gp, SPLITS[0][1], at)
         g_gu = Gather(copy, gg, SPLITS[1][1], at)
@@ -381,8 +382,29 @@
         tok_own = near(tok_ref, tok.at[y])
         tok_own.start()
         cot_own.start()
-        spot_all[y] = spot_ref[...]
-        for cp in stay:
+        spot_all[y] = jnp.broadcast_to(spot_ref[...].astype(F32), (8, rows))
+
+        gain_one, gain_two = gain_ref[:, 0:1].astype(F32), gain_ref[:, 1:2].astype(F32)
+        low_lanes = lax.broadcasted_iota(jnp.int32, (16, 128), 1) < 64
+        for k in range(TP):
+            qs = pl.ds(k * Q_COLS, Q_COLS)
+            wp[k, :, pl.ds(0, Q_COLS)] = (in_ref[:, qs].astype(F32) * gain_one).astype(BF16)
+            key = in_ref[:, pl.ds(D + (k // 2) * 128, 128)].astype(F32)
+            value = in_ref[:, pl.ds(D + HEAD_DIM * KV_HEADS + (k // 2) * 128, 128)].astype(F32)
+            if k % 2 == 0:
+                both = jnp.where(low_lanes, key, pltpu.roll(value, 64, 1))
+            else:
+                both = jnp.where(low_lanes, pltpu.roll(key, 64, 1), value)
+            wp[k, :, pl.ds(Q_COLS, 128)] = (both * gain_one).astype(BF16)
+        stay[0].start()
+        for k in range(TP):
+            for j in range(HID // 128):
+                for half in range(2):
+                    cols = pl.ds(half * FF + k * HID + j * 128, 128)
+                    tile = (mlp_ref[:, cols].astype(F32) * gain_two).astype(BF16)
+                    wg[k, :, pl.ds(j * 256 + half * 128, 128)] = tile
+            wd[k] = down_ref[:, pl.ds(k * HID, HID)]
+        for cp in stay[1:]:
             cp.start()
         meet(ALL_LINES, True)
         away = y != z
@@ -479,6 +501,9 @@
         normed_save = near(normed, normed_out)
         normed_save.start()
 
+        g_gu.turn(0)
+        g_down.turn(0)
+
         wp_load.wait()
         left = normed[...].reshape(count, D)
         lane = lax.broadcasted_iota(jnp.int32, (count, 128), 1)
@@ -488,8 +513,8 @@
         kv[1] = turned.astype(BF16)
         kv_copy.start()
         g_out.far()
-        g_gu.turn()
-        g_down.turn()
+        g_gu.turn(1)
+        g_down.turn(1)
         for j in range(2):
             raw2 = dot(left, wp_v[:, :, :, :, pl.ds(j * 256, 256)].reshape(D, 256))
             for e in range(2):
@@ -549,33 +574,38 @@
             cols = pl.ds(j * 512, 512)
             w = wo_v[:, :, :, :, :, cols].reshape(Q_COLS, 512)
             part[:, :, cols] = dot(att[...], w).astype(BF16).reshape(4, rows, 512)
-        branch.start()
+        for branch in branches:
+            branch.start()
         g_gu.pass_on()
         g_down.pass_on()
-        branch.turn()
+        for branch in branches:
+            branch.turn()
         g_gu.near()
         g_down.near()
         cot_ring.near()
         cot_ring.far()
-        branch.finish()
-
-        def mid(r, _):
-            rs = pl.ds(r * 32, 32)
-            v = tok_ref[rs].astype(F32) + branch.rows(rs)
-            middle_out[rs] = v
-            inv = lax.rsqrt(jnp.mean(v * v, -1, keepdims=True) + EPS)
-            own_two[rs] = (v * inv).astype(BF16)
-            return 0
-
-        lax.fori_loop(0, rows // 32, mid, 0)
         two_own = near(own_two, two_all.at[y])
+        for k in range(2):
+            branches[k].finish()
+
+            def mid(r, _, k=k):
+                rs, half = pl.ds(k * (rows // 2) + r * 32, 32), pl.ds(r * 32, 32)
+                v = tok_ref[rs].astype(F32) + branches[k].rows(half)
+                middle_out[rs] = v
+                inv = lax.rsqrt(jnp.mean(v * v, -1, keepdims=True) + EPS)
+                own_two[rs] = (v * inv).astype(BF16)
+                return 0
+
+            lax.fori_loop(0, rows // 64, mid, 0)
+            two_rings[k].start()
         two_own.start()
-        two_ring.start()
-        two_ring.turn()
+        for ring in two_rings:
+            ring.turn()
         g_gu.far()
         g_down.far()
-        two_ring.near()
-        two_ring.far()
+        for ring in two_rings:
+            ring.near()
+            ring.far()
         g_gu.finish()
         g_down.finish()
         for cp in (cot_own, normed_save, q_save, kv_save, att_save, two_own):
@@ -585,7 +615,7 @@
                 cp.wait_send()
         for cp in spot_copies + [kv_copy]:
             cp.wait_send()
-        for thing in (g_proj, g_out, g_gu, g_down, tok_ring, cot_ring, two_ring, branch):
+        for thing in (g_proj, g_out, g_gu, g_down, tok_ring, cot_ring, *two_rings, *branches):
             thing.sent()
 
     anywhere, vmem = pl.BlockSpec(memory_space=pl.ANY), pl.BlockSpec(memory_space=pltpu.VMEM)
@@ -604,13 +634,16 @@
         (struct((rows, D), F32), vmem),
         (struct((4, rows, D)), anywhere),
     ]
-    copies = 9 + 1 + 3 + 6 * 3 + 6 + 1 + 31 * 4
+    copies = 9 + 1 + 3 + 6 * 6 + 1 + 31 * 4
     return pl.pallas_call(
         kernel,
         out_shape=[o[0] for o in outs],
-        in_specs=[vmem] * 8,
+        in_specs=[vmem] * 9,
         out_specs=[o[1] for o in outs],
         scratch_shapes=[
+            pltpu.VMEM((TP, 16, PROJ), BF16),
+            pltpu.VMEM((TP, 16, 2 * HID), BF16),
+            pltpu.VMEM((TP, 16, HID), BF16),
             pltpu.VMEM((4, rows, D), BF16),
             pltpu.VMEM((4, rows, D), BF16),
             pltpu.VMEM((4, 2, 2, 128, PROJ), BF16),
@@ -633,7 +666,7 @@
         compiler_params=pltpu.CompilerParams(
             collective_id=ident, has_side_effects=True, vmem_limit_bytes=VMEM_LIMIT
         ),
-    )(tokens, cotangent, spots, freqs, w_proj, w_gu, w_down, out_rows)
+    )(tokens, cotangent, positions, freqs, gains, attn_in, mlp_in, mlp_down, out_rows)
 
 
 def tiles(ref):
@@ -837,10 +870,10 @@
     scale = HEAD_DIM ** (-0.5)
 
     def kernel(
-        gu_a_ref, gu_b_ref, s_down, op_ref, br_ref, gm_ref, mid_ref, tok_ref, freq_ref,
+        gu_a_ref, gu_b_ref, s_down, op_ref, br_ref, gm_hbm, mid_hbm, tok_hbm, freq_ref,
         spot_ref, q_ref, kv_ref, att_ref, lse_ref, nm_ref, wp_ref, wo_ref,
         out_ref, ig_ref, o_proj, o_gu, o_down, o_out,
-        v_gu_a, v_gu_b, v_down, part, halves, whole, halves2, whole2, br, q_s, do_s, kv, kvt, att, delta, bias, cos_s, sin_s,
+        gm_ref, mid_ref, tok_ref, v_gu_a, v_gu_b, v_down, part, halves, whole, halves2, whole2, br, q_s, do_s, kv, kvt, att, delta, bias, cos_s, sin_s,
         dkv, kv_send, kv_in, gp, normed, wp, wo, t_proj, rc_proj, t_out, rc_out, *rest,
     ):
         bufs, (send, recv, local) = rest[:24], rest[24:]
@@ -860,7 +893,8 @@
         load_att, load_q = near(att_ref, att), near(q_ref, q_s)
         load_kv = near(kv_ref, kv)
         load_nm, load_wp = near(nm_ref, normed), near(wp_ref, wp)
-        for cp in (load_br, load_wo, load_gu, load_gu_b, load_op, load_down, load_att, load_q, load_kv, load_nm, load_wp):
+        load_rows = [near(gm_hbm, gm_ref), near(mid_hbm, mid_ref), near(tok_hbm, tok_ref)]
+        for cp in (load_br, load_wo, load_gu, load_gu_b, load_op, load_down, load_att, load_q, load_kv, load_nm, load_wp, *load_rows):
             cp.start()
         outs = RingSum(copy, part, halves, whole, y)
         ones = RingSum(copy, part, halves2, whole2, y)
@@ -915,8 +949,9 @@
         load_att.wait()
         lane = lax.broadcasted_iota(jnp.int32, (count, 128), 1)
         for p in range(4):
-            w = wo[p // 2, p % 2].reshape(128, D)
-            low = dot(br[...].reshape(count, D), w, NT).astype(BF16).astype(F32)
+            if p % 2 == 0:
+                both = dot(br[...].reshape(count, D), wo[p // 2].reshape(256, D), NT).astype(BF16).astype(F32)
+            low = both[:, p % 2 * 128 : p % 2 * 128 + 128]
             do_s[2 * p] = jnp.where(lane < 64, 0.0, pltpu.roll(low, 64, 1)).astype(BF16)
             do_s[2 * p + 1] = jnp.where(lane < 64, 0.0, low).astype(BF16)
             prod = jnp.transpose(low * att[:, pl.ds(p * 128, 128)].astype(F32))
@@ -973,6 +1008,9 @@
         down_owners.start()
         outs.finish()
 
+        for cp in load_rows:
+            cp.wait()
+
         def finish_out(r, _):
             rs = pl.ds(r * 32, 32)
             out_ref[rs] = (mid_ref[rs] + outs.rows(rs)).astype(BF16)
@@ -985,16 +1023,17 @@
         back = got * cos_s[...] - swap_halves(got) * sin_s[...]
         gp[:, pl.ds(Q_COLS, 128)] = jnp.where(lane < 64, back, got).astype(BF16)
 
+        load_nm.wait()
+        for k in range(4):
+            left = normed[:, :, pl.ds(k * 512, 512)].reshape(count, 512)
+            t_proj[k] = dot(left, gp[...], TN).astype(BF16).reshape(2, 2, 128, PROJ)
+        core_proj.start()
+
         load_wp.wait()
         for j in range(4):
             w = wp[j].reshape(512, PROJ)
             part[:, :, pl.ds(j * 512, 512)] = dot(gp[...], w, NT).astype(BF16).reshape(4, rows, 512)
         ones.start()
-        load_nm.wait()
-        for k in range(4):
-            left = normed[:, :, pl.ds(k * 512, 512)].reshape(count, 512)
-            t_proj[k] = dot(left, gp[...], TN).astype(BF16).reshape(2, 2, 128, PROJ)
-        core_proj.start()
         out_lines.turn()
         ones.turn()
         down_owners.deliver()
@@ -1030,7 +1069,7 @@
             lines.sent()
 
     anywhere, vmem = pl.BlockSpec(memory_space=pl.ANY), pl.BlockSpec(memory_space=pltpu.VMEM)
-    in_specs = [anywhere] * 5 + [vmem] * 5 + [anywhere] * 3 + [vmem] + [anywhere] * 3
+    in_specs = [anywhere] * 8 + [vmem] * 2 + [anywhere] * 3 + [vmem] + [anywhere] * 3
     outs = [
         (struct((rows, D)), vmem),
         (struct((rows, D), F32), vmem),
@@ -1047,6 +1086,9 @@
         in_specs=in_specs,
         out_specs=[o[1] for o in outs],
         scratch_shapes=[
+            pltpu.VMEM((rows, D), F32),
+            pltpu.VMEM((rows, D), F32),
+            pltpu.VMEM((rows, D), BF16),
             pltpu.VMEM((2, 128, SPLITS[1][1]), BF16),
             pltpu.VMEM((4, 64, 2 * HID - SPLITS[1][1]), BF16),
             pltpu.VMEM((4, 2, 128, HID), BF16),
@@ -1083,7 +1125,7 @@
             *owner_buffers(D, OUT_SPLIT, True),
             pltpu.SemaphoreType.DMA((copies,)),
             pltpu.SemaphoreType.DMA((copies,)),
-            pltpu.SemaphoreType.DMA((16,)),
+            pltpu.SemaphoreType.DMA((20,)),
         ],
         name="backward_attention",
         compiler_params=pltpu.CompilerParams(
@@ -1101,9 +1143,10 @@
     tiles_gu, pairs = HID // 128, HID // 256
 
     def kernel(
-        two_ref, cot_ref, wg_ref, wd_ref, mid_ref, own_cot,
+        two_ref, cot_ref, wg_ref, wd_ref, mid_hbm, own_cot_hbm,
         branch_all, gm_ref, gu_a, gu_b, s_down, op_out,
         part, halves, whole, two, gu, cot, hid, gh, turned, t_gu, t_down, rc_gu, rc_down, branch, op,
+        mid_ref, own_cot,
         far_a, near_a, far_b, near_b, send, recv, local, weights,
     ):
         partners = [along_y(1), along_y(3), along_x(1), along_x(3), along_z(1), along_z(3), sibling]
@@ -1129,6 +1172,7 @@
             )
 
         load_cot, load_two = near(cot_ref, cot), near(two_ref, two)
+        load_rows = [near(mid_hbm, mid_ref), near(own_cot_hbm, own_cot)]
         load_cot.start()
         last_down = load_down(pairs, HID - 256 * pairs)
 
@@ -1144,18 +1188,21 @@
         last_down.start()
         load_two.start()
         lax.fori_loop(0, tiles_gu, begin_gu, 0)
-        ring = RingSum(copy, part, halves, whole, y)
-        gather = RingGather(copy, branch, branch_all, y)
+        for cp in load_rows:
+            cp.start()
+        row_halves = [pl.ds(0, rows // 2), pl.ds(rows // 2, rows // 2)]
+        rings = [RingSum(copy, part.at[:, r], halves.at[:, r], whole.at[:, r], y) for r in row_halves]
+        gathers = [RingGather(copy, branch.at[r], branch_all.at[:, r], y) for r in row_halves]
         own = near(branch, branch_all.at[y])
         cores = [
             (copy(t_gu.at[k, :, 1 - c], rc_gu.at[k], sibling), copy(t_down.at[k, :, 1 - c], rc_down.at[k], sibling))
-            for k in range(4)
+            for k in [(z + d) % 4 for d in range(4)]
         ]
-        saves = [near(t_down.at[k, :, c], s_down.at[k]) for k in range(4)]
+        saves = [near(t_down.at[k, :, c], s_down.at[k]) for k in [(z + d) % 4 for d in range(4)]]
         lines = GradLines(copy, t_gu, SPLITS[1][1], at, (far_a, near_a, far_b, near_b))
         saves_gu = [
-            near(t_gu.at[z, :, c, :, pl.ds(0, HID)], gu_a),
-            near(t_gu.at[:, xh, c, pl.ds(xl * 64, 64), pl.ds(HID, HID)], gu_b),
+            near(t_gu.at[z, :, c, :, pl.ds(0, SPLITS[1][1])], gu_a),
+            near(t_gu.at[:, xh, c, pl.ds(xl * 64, 64), pl.ds(SPLITS[1][1], 2 * HID - SPLITS[1][1])], gu_b),
         ]
         save_op = near(op, op_out)
         load_cot.wait()
@@ -1172,18 +1219,24 @@
         gh[:, tile] = dot(cot[...].reshape(count, D), t_down[:, :, :, :, tile].reshape(D, HID - 256 * pairs))
         load_two.wait()
 
-        def hidden(j, _):
+        def gate_up(j):
             load_gu(j).wait()
             both = pl.ds(pl.multiple_of(j * 256, 256), 256)
+            return dot(two[...].reshape(count, D), t_gu[:, :, :, :, both].reshape(D, 256))
+
+        def activate(j, act):
+            both = pl.ds(pl.multiple_of(j * 256, 256), 256)
             one = pl.ds(pl.multiple_of(j * 128, 128), 128)
-            gate_up = dot(two[...].reshape(count, D), t_gu[:, :, :, :, both].reshape(D, 256))
-            gate, up = gate_up[:, :128], gate_up[:, 128:]
+            gate, up = act[:, :128], act[:, 128:]
             back = gh[:, one]
             sigmoid = jax.nn.sigmoid(gate)
             silu = gate * sigmoid
             hid[:, one] = (silu * up).astype(BF16)
             grad_gate = back * up * sigmoid * (1.0 + gate * (1.0 - sigmoid))
             gu[:, both] = jnp.concatenate([grad_gate, back * silu], 1).astype(BF16)
+
+        def hidden(j, _):
+            activate(j, gate_up(j))
             return 0
 
         lax.fori_loop(0, tiles_gu, hidden, 0)
@@ -1195,15 +1248,17 @@
 
         lax.fori_loop(0, 4, part_two, 0)
         meet(partners)
-        ring.start()
+        for ring in rings:
+            ring.start()
 
         def part_out(k, _):
             cols = pl.ds(pl.multiple_of(k * 512, 512), 512)
             op[:, :, cols] = dot(hid[...], t_down[k].reshape(512, HID), NT).astype(BF16).reshape(4, rows, 512)
             return 0
 
-        def terms_gu(k):
-            cols = pl.ds(k * 512, 512)
+        def terms_gu(d):
+            k = (z + d) % 4
+            cols = pl.ds(pl.multiple_of(k * 512, 512), 512)
             turned[...] = jnp.transpose(two[:, :, cols].reshape(count, 512))
 
             def some(j, _):
@@ -1212,10 +1267,11 @@
                 return 0
 
             lax.fori_loop(0, 2 * HID // 256, some, 0)
-            cores[k][0].start()
-
-        def terms_down(k):
-            cols = pl.ds(k * 512, 512)
+            cores[d][0].start()
+
+        def terms_down(d):
+            k = (z + d) % 4
+            cols = pl.ds(pl.multiple_of(k * 512, 512), 512)
             turned[...] = jnp.transpose(cot[:, :, cols].reshape(count, 512))
 
             def more(j, width=256):
@@ -1225,45 +1281,65 @@
 
             lax.fori_loop(0, pairs, lambda j, _: more(j), 0)
             more(pairs, HID - 256 * pairs)
-            cores[k][1].start()
-
+            cores[d][1].start()
+
+        def add_gu(d):
+            k = (z + d) % 4
+            cores[d][0].wait_recv()
+            add_up(t_gu.at[k, :, c], rc_gu.at[k])
+
+        line_a, line_b = lines.lines
+        terms_gu(2)
+        terms_gu(1)
+        for ring in rings:
+            ring.turn()
+        add_gu(2)
+        for cp in line_a.far:
+            cp.start()
+        terms_gu(3)
+        add_gu(1)
         terms_gu(0)
-        ring.turn()
-        for k in (1, 2, 3):
-            terms_gu(k)
-        for k in range(4):
-            cores[k][0].wait_recv()
-            add_up(t_gu.at[k, :, c], rc_gu.at[k])
-        lines.start()
-        ring.finish()
-
-        def back(r, _):
-            rs = pl.ds(r * 32, 32)
-            v = mid_ref[rs]
-            inv = lax.rsqrt(jnp.mean(v * v, -1, keepdims=True) + EPS)
-            v = v * inv
-            g = ring.rows(rs)
-            value = own_cot[rs].astype(F32) + inv * (g - v * jnp.mean(g * v, -1, keepdims=True))
-            gm_ref[rs] = value
-            branch[rs] = value.astype(BF16)
-            return 0
-
-        lax.fori_loop(0, rows // 32, back, 0)
-        gather.start()
+        add_gu(3)
+        for cp in line_a.near:
+            cp.start()
+        add_gu(0)
+        line_b.start()
+        for cp in load_rows:
+            cp.wait()
+        for k in range(2):
+            rings[k].finish()
+
+            def back(r, _, k=k):
+                rs, half = pl.ds(k * (rows // 2) + r * 32, 32), pl.ds(r * 32, 32)
+                v = mid_ref[rs]
+                inv = lax.rsqrt(jnp.mean(v * v, -1, keepdims=True) + EPS)
+                v = v * inv
+                g = rings[k].rows(half)
+                value = own_cot[rs].astype(F32) + inv * (g - v * jnp.mean(g * v, -1, keepdims=True))
+                gm_ref[rs] = value
+                branch[rs] = value.astype(BF16)
+                return 0
+
+            lax.fori_loop(0, rows // 64, back, 0)
+            gathers[k].start()
         own.start()
         lax.fori_loop(0, 4, part_out, 0)
         save_op.start()
-        gather.turn()
+        for gather in gathers:
+            gather.turn()
+        line_a.turn()
+        terms_down(2)
+        terms_down(1)
+        line_b.turn()
+        terms_down(3)
         terms_down(0)
-        lines.turn()
-        for k in (1, 2, 3):
-            terms_down(k)
-        for k in range(4):
-            cores[k][1].wait_recv()
-            add_up(t_down.at[k, :, c], rc_down.at[k])
-            saves[k].start()
-        gather.near()
-        gather.far()
+        for d in (2, 1, 3, 0):
+            cores[d][1].wait_recv()
+            add_up(t_down.at[(z + d) % 4, :, c], rc_down.at[(z + d) % 4])
+            saves[d].start()
+        for gather in gathers:
+            gather.near()
+            gather.far()
         lines.finish()
         for cp in saves_gu:
             cp.start()
@@ -1275,22 +1351,22 @@
             for cp in pair:
                 cp.wait_send()
         lines.sent()
-        ring.sent()
-        gather.sent()
+        for ring in rings + gathers:
+            ring.sent()
 
     anywhere, vmem = pl.BlockSpec(memory_space=pl.ANY), pl.BlockSpec(memory_space=pltpu.VMEM)
-    copies = 12 + 8 + 12
+    copies = 24 + 8 + 12
     return pl.pallas_call(
         kernel,
         out_shape=[
             struct((4, rows, D)),
             struct((rows, D), F32),
-            struct((2, 128, HID)),
-            struct((4, 64, HID)),
+            struct((2, 128, SPLITS[1][1])),
+            struct((4, 64, 2 * HID - SPLITS[1][1])),
             struct((4, 2, 128, HID)),
             struct((4, rows, D)),
         ],
-        in_specs=[anywhere] * 4 + [vmem] * 2,
+        in_specs=[anywhere] * 6,
         out_specs=[anywhere, vmem, anywhere, anywhere, anywhere, anywhere],
         scratch_shapes=[
             pltpu.VMEM((4, rows, D), BF16),
@@ -1308,10 +1384,12 @@
             pltpu.VMEM((4, 2, 128, HID), BF16),
             pltpu.VMEM((rows, D), BF16),
             pltpu.VMEM((4, rows, D), BF16),
+            pltpu.VMEM((rows, D), F32),
+            pltpu.VMEM((rows, D), BF16),
             *line_buffers(2 * HID, SPLITS[1][1]),
             pltpu.SemaphoreType.DMA((copies,)),
             pltpu.SemaphoreType.DMA((copies,)),
-            pltpu.SemaphoreType.DMA((14,)),
+            pltpu.SemaphoreType.DMA((16,)),
             pltpu.SemaphoreType.DMA((tiles_gu + pairs + 1,)),
         ],
         name="feed_forward",
@@ -1321,32 +1399,61 @@
     )(seq_two, seq_cot, gu_w, down_w, middle, cotangent)
 
 
+def own_rows(gains, attn_in, mlp_in, proj, gu, down, out):
+    def kernel(gain_ref, in_ref, mlp_ref, proj_ref, gu_ref, down_ref, out_ref, g_in, g_mlp, g_down, g_out, g_gain):
+        gain_one, gain_two = gain_ref[:, 0:1].astype(F32), gain_ref[:, 1:2].astype(F32)
+        lane = lax.broadcasted_iota(jnp.int32, (16, 128), 1)
+        low = lane < 64
+
+        def put(dst, weights, at, value, gain, total):
+            cols = pl.ds(at, 128)
+            dst[:, cols] = value * gain
+            return total + value * weights[:, cols].astype(F32)
+
+        first = jnp.zeros((16, 128), F32)
+        for k in range(TP):
+            for j in range(Q_COLS // 128):
+                value = proj_ref[k, :, pl.ds(j * 128, 128)].astype(F32)
+                first = put(g_in, in_ref, k * Q_COLS + j * 128, value, gain_one, first)
+        for k in range(0, TP, 2):
+            even = proj_ref[k, :, pl.ds(Q_COLS, 128)].astype(F32)
+            odd = proj_ref[k + 1, :, pl.ds(Q_COLS, 128)].astype(F32)
+            key = jnp.where(low, even, pltpu.roll(odd, 64, 1))
+            value = jnp.where(low, pltpu.roll(even, 64, 1), odd)
+            first = put(g_in, in_ref, D + k * 64, key, gain_one, first)
+            first = put(g_in, in_ref, D + HEAD_DIM * KV_HEADS + k * 64, value, gain_one, first)
+        second = jnp.zeros((16, 128), F32)
+        for k in range(TP):
+            for j in range(HID // 128):
+                for half in range(2):
+                    value = gu_ref[k, :, pl.ds(j * 256 + half * 128, 128)].astype(F32)
+                    second = put(g_mlp, mlp_ref, half * FF + k * HID + j * 128, value, gain_two, second)
+            g_down[:, pl.ds(k * HID, HID)] = down_ref[k].astype(F32)
+        g_out[...] = out_ref[...].astype(F32)
+        sums = jnp.sum(first, -1, keepdims=True), jnp.sum(second, -1, keepdims=True)
+        g_gain[...] = jnp.transpose(jnp.where(lane == 0, sums[0], sums[1]))[0:8]
+
+    shapes = [(16, attn_in.shape[1]), (16, 2 * FF), (16, FF), (16, D), (8, 16)]
+    return pl.pallas_call(
+        kernel,
+        out_shape=[struct(shape, F32) for shape in shapes],
+        in_specs=[pl.BlockSpec(memory_space=pltpu.VMEM)] * 7,
+        out_specs=[pl.BlockSpec(memory_space=pltpu.VMEM)] * 5,
+        name="own_rows",
+        compiler_params=pltpu.CompilerParams(vmem_limit_bytes=VMEM_LIMIT),
+    )(gains, attn_in, mlp_in, proj, gu, down, out)
+
+
 def shards(tokens, positions, attn_in, attn_out, attn_gain, mlp_in, mlp_down, mlp_gain, cotangent):
-    xh, xl, y, z, c = place()
     rows = tokens.shape[0]
     count = 4 * rows
-    gain_one = attn_gain.astype(F32)[:, None]
-    gain_two = mlp_gain.astype(F32)[:, None]
-
-    in_f = attn_in.astype(F32)
-    mlp_f = mlp_in.astype(F32)
-    kv = HEAD_DIM * KV_HEADS
-    by_y = lambda a: a.reshape(16, TP, -1)
-    w_proj = jnp.concatenate(
-        [by_y(in_f[:, :D]), by_y(in_f[:, D : D + kv]), by_y(in_f[:, D + kv :])], -1
-    )
-    w_proj = (w_proj * gain_one[:, :, None]).astype(BF16).transpose(1, 0, 2)
-    by_tile = lambda a: a.reshape(16, TP, HID // 128, 1, 128)
-    w_gu = jnp.concatenate([by_tile(mlp_f[:, :FF]), by_tile(mlp_f[:, FF:])], 3).reshape(16, TP, 2 * HID)
-    w_gu = (w_gu * gain_two[:, :, None]).astype(BF16).transpose(1, 0, 2)
-    w_down = by_y(mlp_down).transpose(1, 0, 2)
-    spots = jnp.broadcast_to(positions.astype(F32)[None, :], (8, rows))
-    lanes = jnp.arange(128)
-    inv_freq = ROPE_BASE ** (-2.0 * (lanes % 32).astype(F32) / HEAD_DIM)
-    signs = jnp.where(lanes % 64 < 32, -1.0, 1.0)
-    freqs = jnp.zeros((8, 128), F32).at[0].set(inv_freq).at[1].set(signs)
+    gains = jnp.stack([attn_gain, mlp_gain], 1)
+    lanes = np.arange(128)
+    freqs = np.zeros((8, 128), np.float32)
+    freqs[0] = np.float32(ROPE_BASE) ** (-2.0 * (lanes % 32).astype(np.float32) / HEAD_DIM)
+    freqs[1] = np.where(lanes % 64 < 32, -1.0, 1.0)
     (normed_one_all, cot_all, proj_w, gu_w, down_w, out_w, q_all, kv_all, attended_low, lse, spots_all, middle, two_all) = (
-        forward_attention(tokens, cotangent, spots, freqs, w_proj, w_gu, w_down, attn_out, 0)
+        forward_attention(tokens, cotangent, positions[None], freqs, gains, attn_in, mlp_in, mlp_down, attn_out, 0)
     )
     branch_all, grad_middle, gu_a, gu_b, sum_down, out_part = feed_forward(
         two_all, cot_all, gu_w, down_w, middle, cotangent, 1
@@ -1355,28 +1462,10 @@
         gu_a, gu_b, sum_down, out_part, branch_all, grad_middle, middle, tokens, freqs,
         spots_all, q_all, kv_all.reshape(2 * count, 128), attended_low, lse, normed_one_all, proj_w, out_w, 2,
     )
-    own_proj = own_proj.astype(F32).transpose(1, 0, 2)
-    cut = lambda a, start, stop: a[:, :, start:stop].reshape(16, -1)
-    own_proj = jnp.concatenate(
-        [
-            cut(own_proj, 0, Q_COLS),
-            cut(own_proj, Q_COLS, Q_COLS + HEAD_DIM),
-            cut(own_proj, Q_COLS + HEAD_DIM, PROJ),
-        ],
-        -1,
+    grad_in, grad_mlp, grad_down, grad_out, grad_gains = own_rows(
+        gains, attn_in, mlp_in, own_proj, own_gu, own_down, own_out
     )
-    own_gu = own_gu.reshape(TP, 16, HID // 128, 2, 128).transpose(1, 3, 0, 2, 4).reshape(16, 2 * FF).astype(F32)
-    own_down = own_down.astype(F32).transpose(1, 0, 2).reshape(16, FF)
-    return (
-        outputs,
-        input_grad,
-        own_proj * gain_one,
-        own_out.astype(F32),
-        jnp.sum(own_proj * in_f, -1),
-        own_gu * gain_two,
-        own_down,
-        jnp.sum(own_gu * mlp_f, -1),
-    )
+    return outputs, input_grad, grad_in, grad_out, grad_gains[0], grad_mlp, grad_down, grad_gains[1]
 
 
 def solution(mesh):

time: 264 us -> 243 us (0.920); the launches traced: 261 us -> 242 us
  other arithmetic: 9.08 us -> 0.68 us
  local copies, waits for them, and re-layouts: 10.2 us -> 4.82 us
  Pallas kernels: 240 us -> 236 us
    pallas_call x1, Pallas kernels: 102 us -> 97.8 us  [forward_attention(): pl.pallas_call(kernel, out_shape=[o[0] for o in outs], in_specs=[vmem] *...]
    convert_element_type x4 -> x0, other arithmetic: 3.53 us -> none  [the longest x1 1.56 us: shards(): own_out.astype(F32)]
    reshape x13 -> x0, local copies, waits for them, and re-layouts: 3.5 us -> none  [the longest x6 1.79 us: shards(): by_y = lambda a: a.reshape(16, TP, -1)]
    reduce_sum x2 -> x0, other arithmetic: 2.97 us -> none  [the longest x1 1.6 us: shards(): jnp.sum(own_gu * mlp_f, -1)]
    slice x6 -> x0, local copies, waits for them, and re-layouts: 2.73 us -> none  [the longest x1 1.06 us: shards(): mlp_f[:, :FF]]
    pallas_call x0 -> x1, Pallas kernels: none -> 2.7 us  [own_rows(): pl.pallas_call(kernel, out_shape=[struct(shape, F32) for shape in shapes]...]
where the time goes in v1:
time: 243 us; the launch traced here: 242 us
  Pallas kernels  236 us (97%)
  local copies, waits for them, and re-layouts  4.82 us (2%)
    pallas_call x1, Pallas kernels, forward_attention(): pl.pallas_call(kernel, out_shape=[o[0] for o in outs], in_specs=[vmem] *...  97.8 us
    pallas_call x1, Pallas kernels, feed_forward(): pl.pallas_call(kernel, out_shape=[struct((4, rows, D)), struct((rows, D),...  70.2 us
    pallas_call x1, Pallas kernels, backward_attention(): pl.pallas_call(kernel, out_shape=[o[0] for o in outs], in_specs=in_specs,...  65.4 us

profile of v1, /device:TPU:0, one launch (start us, length us, event | category | flops | bytes accessed | tf_op | source)
XLA Modules:
  0.0 242.3 jit_solution(10352460991316316530)
XLA Ops:
  0.6 0.7 pad_maximum_fusion
  1.3 0.7 copy.20.gain_ref
  2.0 97.8 %forward_attention.1 = (bf16[4,128,2048]{2,1,0:T(8,128)(2,1)}, bf16[4,128,2048]{2,1,0:T(8,128)(2,1)}, bf16[4,2,2,128,640]{4,3,2,1,0:T(8,128)(2,1)}, bf16[4,2,2,1...) custom-call(bf16[128,2048]{1,0:T(8,128)(2,1)} %tok_hbm.1, ...), custom_call_target="tpu_custom_call" | custom-call | tf_op jit(solution)/shard_map/forward_attention/pallas_call | solution.py:638
  99.9 70.2 %feed_forward.1 = (bf16[4,128,2048]{2,1,0:T(8,128)(2,1)}, f32[128,2048]{1,0:T(8,128)}, bf16[2,128,1664]{2,1,0:T(8,128)(2,1)}, bf16[4,64,1152]{2,1,0:T(8,128)(2,1...) custom-call(bf16[4,128,2048]{2,1,0:T(8,128)(2,1)} %get-tuple-element.38.two_ref, ...), custom_call_target="tpu_custom_call" | custom-call | tf_op jit(solution)/shard_map/feed_forward/pallas_call | solution.py:1359
  170.0 65.4 %backward_attention.1 = (bf16[128,2048]{1,0:T(8,128)(2,1)}, f32[128,2048]{1,0:T(8,128)}, bf16[4,16,640]{2,1,0:T(8,128)(2,1)}, bf16[4,16,2816]{2,1,0:T(8,128)(2,1...) custom-call(bf16[2,128,1664]{2,1,0:T(8,128)(2,1)} %get-tuple-element.43.gu_a_ref, ...), custom_call_target="tpu_custom_call" | custom-call | tf_op jit(solution)/shard_map/backward_attention/pallas_call | solution.py:1083
  235.5 0.0 copy-start
  235.5 2.7 %own_rows.1 = (f32[16,2560]{1,0:T(8,128)}, f32[16,11264]{1,0:T(8,128)}, f32[16,5632]{1,0:T(8,128)}, f32[16,2048]{1,0:T(8,128)}, f32[8,16]{1,0:T(8,128)}) custom-call(bf16[16,2]{1,0:T(8,128)(2,1)} %copy.20.gain_ref, bf16[16,2560]{1,0:T(8,128)(2,1)} %in_ref.3, bf16[16,11264]{1,0:T(8,128)(2,1)} %mlp_ref.3, bf16[4,16,640]{2,1,0:T(8,128)(2,1)} %get-tuple-element.59.proj_ref, ...), custom_call_target="tpu_custom_call" | custom-call | tf_op jit(solution)/shard_map/own_rows/pallas_call | solution.py:1437
  238.2 1.3 slice_bitcast_fusion
  239.5 1.9 copy.24
  241.3 0.0 copy-done
  241.3 1.0 copy.25
Async XLA Ops:
  235.5 5.9 %copy-start = (f32[128,2048]{1,0:T(8,128)S(1)}, f32[128,2048]{1,0:T(8,128)}, u32[]{:S(2)}) copy-start(f32[128,2048]{1,0:T(8,128)} %get-tuple-element.79) | copy-start | bytes 3145732

commit v2 on v1

--- a/solution.py
+++ b/solution.py
@@ -344,8 +344,8 @@
 
     def kernel(
         tok_ref, cot_ref, spot_ref, freq_ref, gain_ref, in_ref, mlp_ref, down_ref, wo,
-        normed_out, cot_all, gp, gg, gd, go, q_out, kv_out, att_out, lse_out, spot_out, middle_out, two_all,
-        wp, wg, wd, tok, normed, wp_v, wo_v, q_s, kv, vx, bias, att, part, halves, whole, spot_all, own_two, send, recv, local,
+        normed_out, cot_all, gp, gg, gd, go, q_out, kv_out, att_out, lse_out, cos_out, sin_out, bias_out, middle_out, two_all,
+        wp, wg, wd, tok, normed, wp_v, wo_v, q_s, kv, vx, bias, att, part, halves, whole, spot_all, own_two, cos_s, sin_s, bias_t, send, recv, local,
     ):
         say_hello(ALL_LINES, True)
         at = place()
@@ -450,12 +450,14 @@
         norm_block(y)
         g_proj.turn()
         stay[1].wait()
-        stay[2].wait()
-        for cp in to_y[1] + to_y[2]:
+        for cp in to_y[1]:
             cp.wait_recv()
         g_gu.start()
+        g_proj.pass_on()
+        stay[2].wait()
+        for cp in to_y[2]:
+            cp.wait_recv()
         g_down.start()
-        g_proj.pass_on()
         g_out.turn()
         for cp in spot_copies:
             cp.wait_recv()
@@ -468,11 +470,15 @@
         spot_cols = []
         for k in range(4):
             col = jnp.transpose(jnp.broadcast_to(spot_all[k, 0:1, :], (128, 128)))
-            spot_out[k] = spot_all[k]
             spot_cols.append(col)
             cos.append(jnp.cos(col * freq))
             sin.append(jnp.sin(col * freq) * sign)
         cos, sin = jnp.concatenate(cos, 0), jnp.concatenate(sin, 0)
+        cos_s[...] = cos
+        sin_s[...] = sin
+        turn_saves = [near(cos_s, cos_out), near(sin_s, sin_out)]
+        for cp in turn_saves:
+            cp.start()
         low_half = xl == 0
         reach = jnp.where(low_half, -1.0, 2048.0)
         for k in range(4):
@@ -576,6 +582,20 @@
             part[:, :, cols] = dot(att[...], w).astype(BF16).reshape(4, rows, 512)
         for branch in branches:
             branch.start()
+
+        for k in range(4):
+            for j in range(8):
+                key = lax.broadcasted_iota(jnp.int32, (128, 128), 0) + j * 128
+                row = lax.broadcasted_iota(jnp.int32, (128, 128), 1) + k * 128
+                apart = (row - key + 512).astype(F32)
+                seen = apart <= spot_all[k, 0:1, :]
+                if j < 4:
+                    seen = seen & (apart <= reach)
+                else:
+                    seen = seen & (key - 512 <= row)
+                bias_t[pl.ds(j * 128, 128), pl.ds(k * 128, 128)] = jnp.where(seen, 0.0, NEG_FILL)
+        bias_save = near(bias_t, bias_out)
+        bias_save.start()
         g_gu.pass_on()
         g_down.pass_on()
         for branch in branches:
@@ -608,7 +628,7 @@
             ring.far()
         g_gu.finish()
         g_down.finish()
-        for cp in (cot_own, normed_save, q_save, kv_save, att_save, two_own):
+        for cp in (cot_own, normed_save, q_save, kv_save, att_save, two_own, bias_save, *turn_saves):
             cp.wait()
         for group in to_y:
             for cp in group:
@@ -630,7 +650,9 @@
         (struct((2, count, 128)), anywhere),
         (struct((count, Q_COLS)), anywhere),
         (struct((REPEAT, 8, count), F32), vmem),
-        (struct((4, 8, 128), F32), vmem),
+        (struct((count, 128), F32), anywhere),
+        (struct((count, 128), F32), anywhere),
+        (struct((2 * count, count), F32), anywhere),
         (struct((rows, D), F32), vmem),
         (struct((4, rows, D)), anywhere),
     ]
@@ -658,9 +680,12 @@
             pltpu.VMEM((2, rows, D), BF16),
             pltpu.VMEM((4, 8, 128), F32),
             pltpu.VMEM((rows, D), BF16),
+            pltpu.VMEM((count, 128), F32),
+            pltpu.VMEM((count, 128), F32),
+            pltpu.VMEM((2 * count, count), F32),
             pltpu.SemaphoreType.DMA((copies,)),
             pltpu.SemaphoreType.DMA((copies,)),
-            pltpu.SemaphoreType.DMA((16,)),
+            pltpu.SemaphoreType.DMA((20,)),
         ],
         name="forward_attention",
         compiler_params=pltpu.CompilerParams(
@@ -852,28 +877,19 @@
     return [pltpu.VMEM((3, spot, a), BF16), pltpu.VMEM((3, spot, cols - a), BF16), pltpu.VMEM(own, BF16)]
 
 
-def rotation(spot_rows, freq_ref):
-    cos, sin = [], []
-    for k in range(4):
-        col = jnp.transpose(jnp.broadcast_to(spot_rows[k, 0:1, :], (128, 128)))
-        cos.append(jnp.cos(col * freq_ref[0:1, :]))
-        sin.append(jnp.sin(col * freq_ref[0:1, :]) * freq_ref[1:2, :])
-    return jnp.concatenate(cos, 0), jnp.concatenate(sin, 0)
-
-
 def backward_attention(
-    gu_a, gu_b, sum_down, out_part, branch_all, grad_middle, middle, tokens, freqs,
-    spots, q_all, kv_all, attended, lse, normed_all, proj_w, out_w, ident,
+    gu_a, gu_b, sum_down, out_part, branch_all, grad_middle, middle, tokens,
+    cosines, sines, bias_all, q_all, kv_all, attended, lse, normed_all, proj_w, out_w, ident,
 ):
     rows = tokens.shape[0]
     count = 4 * rows
     scale = HEAD_DIM ** (-0.5)
 
     def kernel(
-        gu_a_ref, gu_b_ref, s_down, op_ref, br_ref, gm_hbm, mid_hbm, tok_hbm, freq_ref,
-        spot_ref, q_ref, kv_ref, att_ref, lse_ref, nm_ref, wp_ref, wo_ref,
+        gu_a_ref, gu_b_ref, s_down, op_ref, br_ref, gm_hbm, mid_hbm, tok_hbm,
+        cos_ref, sin_ref, bias_ref, q_ref, kv_ref, att_ref, lse_ref, nm_ref, wp_ref, wo_ref,
         out_ref, ig_ref, o_proj, o_gu, o_down, o_out,
-        gm_ref, mid_ref, tok_ref, v_gu_a, v_gu_b, v_down, part, halves, whole, halves2, whole2, br, q_s, do_s, kv, kvt, att, delta, bias, cos_s, sin_s,
+        gm_ref, mid_ref, tok_ref, v_gu_a, v_gu_b, v_down, part, part_in, halves, whole, halves2, whole2, br, q_s, do_s, kv, kvt, att, delta, bias, cos_s, sin_s,
         dkv, kv_send, kv_in, gp, normed, wp, wo, t_proj, rc_proj, t_out, rc_out, *rest,
     ):
         bufs, (send, recv, local) = rest[:24], rest[24:]
@@ -892,14 +908,18 @@
         load_op, load_br, load_wo = near(op_ref, part), near(br_ref, br), near(wo_ref, wo)
         load_att, load_q = near(att_ref, att), near(q_ref, q_s)
         load_kv = near(kv_ref, kv)
+        load_turns = [near(cos_ref, cos_s), near(sin_ref, sin_s), near(bias_ref, bias)]
         load_nm, load_wp = near(nm_ref, normed), near(wp_ref, wp)
         load_rows = [near(gm_hbm, gm_ref), near(mid_hbm, mid_ref), near(tok_hbm, tok_ref)]
-        for cp in (load_br, load_wo, load_gu, load_gu_b, load_op, load_down, load_att, load_q, load_kv, load_nm, load_wp, *load_rows):
+        for cp in (load_br, load_wo, load_gu, load_gu_b, load_op, load_down, load_att, load_q, load_kv, *load_turns, load_nm, load_wp, *load_rows):
             cp.start()
         outs = RingSum(copy, part, halves, whole, y)
-        ones = RingSum(copy, part, halves2, whole2, y)
+        ones = RingSum(copy, part_in, halves2, whole2, y)
         kv_copy = copy(kv_send, kv_in, half_partner)
-        core_proj = copy(t_proj.at[:, :, 1 - c], rc_proj, sibling)
+        core_proj = [
+            copy(t_proj.at[:, :, 1 - c, :, cols], rc_proj.at[:, :, :, cols], sibling)
+            for cols in (pl.ds(0, Q_COLS), pl.ds(Q_COLS, 128))
+        ]
         core_out = copy(t_out.at[:, 1 - c], rc_out, sibling)
         gu_owners = GradOwners(
             copy,
@@ -917,22 +937,6 @@
         out_lines = GradLines(copy, t_out, OUT_SPLIT, at, bufs[17:21], True)
         out_owners = GradOwners(copy, near, out_lines.spot_a, out_lines.spot_b, o_out, at, bufs[21:24], True)
 
-        cos, sin = rotation(spot_ref, freq_ref)
-        cos_s[...] = cos
-        sin_s[...] = sin
-        reach = jnp.where(xl == 0, -1.0, 2048.0)
-        for k in range(4):
-            spots_row = spot_ref[k, 0:1, :]
-            for j in range(8):
-                key = lax.broadcasted_iota(jnp.int32, (128, 128), 0) + j * 128
-                row = lax.broadcasted_iota(jnp.int32, (128, 128), 1) + k * 128
-                apart = (row - key + 512).astype(F32)
-                seen = apart <= spots_row
-                if j < 4:
-                    seen = seen & (apart <= reach)
-                else:
-                    seen = seen & (key - 512 <= row)
-                bias[pl.ds(j * 128, 128), pl.ds(k * 128, 128)] = jnp.where(seen, 0.0, NEG_FILL)
         dkv[...] = jnp.zeros_like(dkv)
 
         meet(ALL_LINES, True)
@@ -995,6 +999,8 @@
 
             lax.fori_loop(0, 2, body, 0)
 
+        for cp in load_turns:
+            cp.wait()
         two_pairs(0)
         down_lines.turn()
         gu_owners.deliver()
@@ -1004,6 +1010,27 @@
         core_out.wait_recv()
         add_up(t_out.at[:, c], rc_out)
         out_lines.start()
+        load_nm.wait()
+        for k in range(4):
+            left = normed[:, :, pl.ds(k * 512, 512)].reshape(count, 512)
+            term = dot(left, gp[:, pl.ds(0, Q_COLS)], TN)
+            t_proj[k, :, :, :, pl.ds(0, Q_COLS)] = term.astype(BF16).reshape(2, 2, 128, Q_COLS)
+        core_proj[0].start()
+        kv_copy.wait_recv()
+        got = dkv[pl.ds(count, count)] + kv_in[...].astype(F32)
+        back = got * cos_s[...] - swap_halves(got) * sin_s[...]
+        gp[:, pl.ds(Q_COLS, 128)] = jnp.where(lane < 64, back, got).astype(BF16)
+        for k in range(4):
+            left = normed[:, :, pl.ds(k * 512, 512)].reshape(count, 512)
+            term = dot(left, gp[:, pl.ds(Q_COLS, 128)], TN)
+            t_proj[k, :, :, :, pl.ds(Q_COLS, 128)] = term.astype(BF16).reshape(2, 2, 128, 128)
+        core_proj[1].start()
+
+        load_wp.wait()
+        for j in range(4):
+            w = wp[j].reshape(512, PROJ)
+            part_in[:, :, pl.ds(j * 512, 512)] = dot(gp[...], w, NT).astype(BF16).reshape(4, rows, 512)
+        ones.start()
         down_lines.finish()
         down_owners.start()
         outs.finish()
@@ -1018,26 +1045,11 @@
 
         lax.fori_loop(0, rows // 32, finish_out, 0)
         outs.sent()
-        kv_copy.wait_recv()
-        got = dkv[pl.ds(count, count)] + kv_in[...].astype(F32)
-        back = got * cos_s[...] - swap_halves(got) * sin_s[...]
-        gp[:, pl.ds(Q_COLS, 128)] = jnp.where(lane < 64, back, got).astype(BF16)
-
-        load_nm.wait()
-        for k in range(4):
-            left = normed[:, :, pl.ds(k * 512, 512)].reshape(count, 512)
-            t_proj[k] = dot(left, gp[...], TN).astype(BF16).reshape(2, 2, 128, PROJ)
-        core_proj.start()
-
-        load_wp.wait()
-        for j in range(4):
-            w = wp[j].reshape(512, PROJ)
-            part[:, :, pl.ds(j * 512, 512)] = dot(gp[...], w, NT).astype(BF16).reshape(4, rows, 512)
-        ones.start()
         out_lines.turn()
         ones.turn()
         down_owners.deliver()
-        core_proj.wait_recv()
+        for cp in core_proj:
+            cp.wait_recv()
         for k in range(4):
             add_up(t_proj.at[k, :, c], rc_proj.at[k])
         proj_lines.start()
@@ -1061,7 +1073,7 @@
         out_owners.deliver()
         proj_owners.deliver()
         ones.sent()
-        for cp in (kv_copy, core_proj, core_out):
+        for cp in (kv_copy, *core_proj, core_out):
             cp.wait_send()
         for owners in (gu_owners, down_owners, out_owners, proj_owners):
             owners.finish()
@@ -1069,7 +1081,7 @@
             lines.sent()
 
     anywhere, vmem = pl.BlockSpec(memory_space=pl.ANY), pl.BlockSpec(memory_space=pltpu.VMEM)
-    in_specs = [anywhere] * 8 + [vmem] * 2 + [anywhere] * 3 + [vmem] + [anywhere] * 3
+    in_specs = [anywhere] * 14 + [vmem] + [anywhere] * 3
     outs = [
         (struct((rows, D)), vmem),
         (struct((rows, D), F32), vmem),
@@ -1079,7 +1091,7 @@
         (struct((16, D)), anywhere),
     ]
     whole = lambda: [pltpu.VMEM((2, rows, D // 2), BF16), pltpu.VMEM((2, rows, D), BF16)]
-    copies = 12 + 3 + 9 + 21 * 2 + 19
+    copies = 12 + 4 + 9 + 21 * 2 + 19
     return pl.pallas_call(
         kernel,
         out_shape=[o[0] for o in outs],
@@ -1092,6 +1104,7 @@
             pltpu.VMEM((2, 128, SPLITS[1][1]), BF16),
             pltpu.VMEM((4, 64, 2 * HID - SPLITS[1][1]), BF16),
             pltpu.VMEM((4, 2, 128, HID), BF16),
+            pltpu.VMEM((4, rows, D), BF16),
             pltpu.VMEM((4, rows, D), BF16),
             *whole(),
             *whole(),
@@ -1125,15 +1138,15 @@
             *owner_buffers(D, OUT_SPLIT, True),
             pltpu.SemaphoreType.DMA((copies,)),
             pltpu.SemaphoreType.DMA((copies,)),
-            pltpu.SemaphoreType.DMA((20,)),
+            pltpu.SemaphoreType.DMA((24,)),
         ],
         name="backward_attention",
         compiler_params=pltpu.CompilerParams(
             collective_id=ident, has_side_effects=True, vmem_limit_bytes=VMEM_LIMIT
         ),
     )(
-        gu_a, gu_b, sum_down, out_part, branch_all, grad_middle, middle, tokens, freqs,
-        spots, q_all, kv_all, attended, lse, normed_all, proj_w, out_w,
+        gu_a, gu_b, sum_down, out_part, branch_all, grad_middle, middle, tokens,
+        cosines, sines, bias_all, q_all, kv_all, attended, lse, normed_all, proj_w, out_w,
     )
 
 
@@ -1452,15 +1465,15 @@
     freqs = np.zeros((8, 128), np.float32)
     freqs[0] = np.float32(ROPE_BASE) ** (-2.0 * (lanes % 32).astype(np.float32) / HEAD_DIM)
     freqs[1] = np.where(lanes % 64 < 32, -1.0, 1.0)
-    (normed_one_all, cot_all, proj_w, gu_w, down_w, out_w, q_all, kv_all, attended_low, lse, spots_all, middle, two_all) = (
+    (normed_one_all, cot_all, proj_w, gu_w, down_w, out_w, q_all, kv_all, attended_low, lse, cosines, sines, bias_all, middle, two_all) = (
         forward_attention(tokens, cotangent, positions[None], freqs, gains, attn_in, mlp_in, mlp_down, attn_out, 0)
     )
     branch_all, grad_middle, gu_a, gu_b, sum_down, out_part = feed_forward(
         two_all, cot_all, gu_w, down_w, middle, cotangent, 1
     )
     outputs, input_grad, own_proj, own_gu, own_down, own_out = backward_attention(
-        gu_a, gu_b, sum_down, out_part, branch_all, grad_middle, middle, tokens, freqs,
-        spots_all, q_all, kv_all.reshape(2 * count, 128), attended_low, lse, normed_one_all, proj_w, out_w, 2,
+        gu_a, gu_b, sum_down, out_part, branch_all, grad_middle, middle, tokens,
+        cosines, sines, bias_all, q_all, kv_all.reshape(2 * count, 128), attended_low, lse, normed_one_all, proj_w, out_w, 2,
     )
     grad_in, grad_mlp, grad_down, grad_out, grad_gains = own_rows(
         gains, attn_in, mlp_in, own_proj, own_gu, own_down, own_out

time: 243 us -> 240 us (0.988)
  Pallas kernels: 236 us -> 233 us
where the time goes in v2:
time: 240 us; the launch traced here: 239 us
  Pallas kernels  233 us (97%)
  local copies, waits for them, and re-layouts  4.82 us (2%)
    pallas_call x1, Pallas kernels, forward_attention(): pl.pallas_call(kernel, out_shape=[o[0] for o in outs], in_specs=[vmem] *...  95.9 us
    pallas_call x1, Pallas kernels, feed_forward(): pl.pallas_call(kernel, out_shape=[struct((4, rows, D)), struct((rows, D),...  70 us
    pallas_call x1, Pallas kernels, backward_attention(): pl.pallas_call(kernel, out_shape=[o[0] for o in outs], in_specs=in_specs,...  64.2 us

profile of v2, /device:TPU:0, one launch (start us, length us, event | category | flops | bytes accessed | tf_op | source)
XLA Modules:
  0.0 239.0 jit_solution(17675178923489055167)
XLA Ops:
  0.6 0.7 pad_maximum_fusion
  1.3 0.7 copy.20.gain_ref
  2.0 95.9 %forward_attention.1 = (bf16[4,128,2048]{2,1,0:T(8,128)(2,1)}, bf16[4,128,2048]{2,1,0:T(8,128)(2,1)}, bf16[4,2,2,128,640]{4,3,2,1,0:T(8,128)(2,1)}, bf16[4,2,2,1...) custom-call(bf16[128,2048]{1,0:T(8,128)(2,1)} %tok_hbm.1, ...), custom_call_target="tpu_custom_call" | custom-call | tf_op jit(solution)/shard_map/forward_attention/pallas_call | solution.py:660
  98.0 70.0 %feed_forward.1 = (bf16[4,128,2048]{2,1,0:T(8,128)(2,1)}, f32[128,2048]{1,0:T(8,128)}, bf16[2,128,1664]{2,1,0:T(8,128)(2,1)}, bf16[4,64,1152]{2,1,0:T(8,128)(2,1...) custom-call(bf16[4,128,2048]{2,1,0:T(8,128)(2,1)} %get-tuple-element.40.two_ref, ...), custom_call_target="tpu_custom_call" | custom-call | tf_op jit(solution)/shard_map/feed_forward/pallas_call | solution.py:1372
  168.0 64.2 %backward_attention.1 = (bf16[128,2048]{1,0:T(8,128)(2,1)}, f32[128,2048]{1,0:T(8,128)}, bf16[4,16,640]{2,1,0:T(8,128)(2,1)}, bf16[4,16,2816]{2,1,0:T(8,128)(2,1...) custom-call(bf16[2,128,1664]{2,1,0:T(8,128)(2,1)} %get-tuple-element.45.gu_a_ref, ...), custom_call_target="tpu_custom_call" | custom-call | tf_op jit(solution)/shard_map/backward_attention/pallas_call | solution.py:1095
  232.2 0.0 copy-start
  232.2 2.7 %own_rows.1 = (f32[16,2560]{1,0:T(8,128)}, f32[16,11264]{1,0:T(8,128)}, f32[16,5632]{1,0:T(8,128)}, f32[16,2048]{1,0:T(8,128)}, f32[8,16]{1,0:T(8,128)}) custom-call(bf16[16,2]{1,0:T(8,128)(2,1)} %copy.20.gain_ref, bf16[16,2560]{1,0:T(8,128)(2,1)} %in_ref.3, bf16[16,11264]{1,0:T(8,128)(2,1)} %mlp_ref.3, bf16[4,16,640]{2,1,0:T(8,128)(2,1)} %get-tuple-element.63.proj_ref, ...), custom_call_target="tpu_custom_call" | custom-call | tf_op jit(solution)/shard_map/own_rows/pallas_call | solution.py:1450
  234.9 1.3 slice_bitcast_fusion
  236.2 1.9 copy.24
  238.1 0.0 copy-done
  238.1 1.0 copy.25
Async XLA Ops:
  232.2 5.9 %copy-start = (f32[128,2048]{1,0:T(8,128)S(1)}, f32[128,2048]{1,0:T(8,128)}, u32[]{:S(2)}) copy-start(f32[128,2048]{1,0:T(8,128)} %get-tuple-element.83) | copy-start | bytes 3145732

commit v3 on v2

--- a/solution.py
+++ b/solution.py
@@ -333,17 +333,23 @@
     return lax.dot_general(left, right, (dims, ((), ())), preferred_element_type=F32)
 
 
+def column(row_ref):
+    row = jnp.broadcast_to(row_ref[...].astype(F32), (16, 16))
+    diagonal = lax.broadcasted_iota(jnp.int32, (16, 16), 0) == lax.broadcasted_iota(jnp.int32, (16, 16), 1)
+    return jnp.sum(jnp.where(diagonal, row, 0.0), 1, keepdims=True)
+
+
 def swap_halves(v):
     lane = lax.broadcasted_iota(jnp.int32, v.shape, 1)
     return jnp.where(lane % 64 < 32, pltpu.roll(v, 96, 1), pltpu.roll(v, 32, 1))
 
 
-def forward_attention(tokens, cotangent, positions, freqs, gains, attn_in, mlp_in, mlp_down, out_rows, ident):
+def forward_attention(tokens, cotangent, positions, freqs, attn_gain, mlp_gain, attn_in, mlp_in, mlp_down, out_rows, ident):
     rows = tokens.shape[0]
     count = 4 * rows
 
     def kernel(
-        tok_ref, cot_ref, spot_ref, freq_ref, gain_ref, in_ref, mlp_ref, down_ref, wo,
+        tok_ref, cot_ref, spot_ref, freq_ref, one_ref, two_ref, in_ref, mlp_ref, down_ref, wo,
         normed_out, cot_all, gp, gg, gd, go, q_out, kv_out, att_out, lse_out, cos_out, sin_out, bias_out, middle_out, two_all,
         wp, wg, wd, tok, normed, wp_v, wo_v, q_s, kv, vx, bias, att, part, halves, whole, spot_all, own_two, cos_s, sin_s, bias_t, send, recv, local,
     ):
@@ -384,7 +390,7 @@
         cot_own.start()
         spot_all[y] = jnp.broadcast_to(spot_ref[...].astype(F32), (8, rows))
 
-        gain_one, gain_two = gain_ref[:, 0:1].astype(F32), gain_ref[:, 1:2].astype(F32)
+        gain_one, gain_two = column(one_ref), column(two_ref)
         low_lanes = lax.broadcasted_iota(jnp.int32, (16, 128), 1) < 64
         for k in range(TP):
             qs = pl.ds(k * Q_COLS, Q_COLS)
@@ -660,7 +666,7 @@
     return pl.pallas_call(
         kernel,
         out_shape=[o[0] for o in outs],
-        in_specs=[vmem] * 9,
+        in_specs=[vmem] * 10,
         out_specs=[o[1] for o in outs],
         scratch_shapes=[
             pltpu.VMEM((TP, 16, PROJ), BF16),
@@ -691,7 +697,7 @@
         compiler_params=pltpu.CompilerParams(
             collective_id=ident, has_side_effects=True, vmem_limit_bytes=VMEM_LIMIT
         ),
-    )(tokens, cotangent, positions, freqs, gains, attn_in, mlp_in, mlp_down, out_rows)
+    )(tokens, cotangent, positions, freqs, attn_gain, mlp_gain, attn_in, mlp_in, mlp_down, out_rows)
 
 
 def tiles(ref):
@@ -1031,31 +1037,35 @@
             w = wp[j].reshape(512, PROJ)
             part_in[:, :, pl.ds(j * 512, 512)] = dot(gp[...], w, NT).astype(BF16).reshape(4, rows, 512)
         ones.start()
-        down_lines.finish()
-        down_owners.start()
-        outs.finish()
-
-        for cp in load_rows:
-            cp.wait()
-
-        def finish_out(r, _):
-            rs = pl.ds(r * 32, 32)
-            out_ref[rs] = (mid_ref[rs] + outs.rows(rs)).astype(BF16)
-            return 0
-
-        lax.fori_loop(0, rows // 32, finish_out, 0)
-        outs.sent()
-        out_lines.turn()
-        ones.turn()
-        down_owners.deliver()
         for cp in core_proj:
             cp.wait_recv()
         for k in range(4):
             add_up(t_proj.at[k, :, c], rc_proj.at[k])
         proj_lines.start()
+        out_lines.turn()
+        ones.turn()
+        proj_lines.turn()
+        down_lines.finish()
+        down_owners.start()
         out_lines.finish()
         out_owners.start()
-        proj_lines.turn()
+        proj_lines.finish()
+        proj_owners.start()
+        down_owners.deliver()
+        out_owners.deliver()
+        proj_owners.deliver()
+        outs.finish()
+
+        for cp in load_rows:
+            cp.wait()
+
+        def finish_out(r, _):
+            rs = pl.ds(r * 32, 32)
+            out_ref[rs] = (mid_ref[rs] + outs.rows(rs)).astype(BF16)
+            return 0
+
+        lax.fori_loop(0, rows // 32, finish_out, 0)
+        outs.sent()
         ones.finish()
 
         def finish_in(r, _):
@@ -1068,10 +1078,6 @@
             return 0
 
         lax.fori_loop(0, rows // 32, finish_in, 0)
-        proj_lines.finish()
-        proj_owners.start()
-        out_owners.deliver()
-        proj_owners.deliver()
         ones.sent()
         for cp in (kv_copy, *core_proj, core_out):
             cp.wait_send()
@@ -1412,9 +1418,9 @@
     )(seq_two, seq_cot, gu_w, down_w, middle, cotangent)
 
 
-def own_rows(gains, attn_in, mlp_in, proj, gu, down, out):
-    def kernel(gain_ref, in_ref, mlp_ref, proj_ref, gu_ref, down_ref, out_ref, g_in, g_mlp, g_down, g_out, g_gain):
-        gain_one, gain_two = gain_ref[:, 0:1].astype(F32), gain_ref[:, 1:2].astype(F32)
+def own_rows(attn_gain, mlp_gain, attn_in, mlp_in, proj, gu, down, out):
+    def kernel(one_ref, two_ref, in_ref, mlp_ref, proj_ref, gu_ref, down_ref, out_ref, g_in, g_mlp, g_down, g_out, g_gain):
+        gain_one, gain_two = column(one_ref), column(two_ref)
         lane = lax.broadcasted_iota(jnp.int32, (16, 128), 1)
         low = lane < 64
 
@@ -1450,23 +1456,23 @@
     return pl.pallas_call(
         kernel,
         out_shape=[struct(shape, F32) for shape in shapes],
-        in_specs=[pl.BlockSpec(memory_space=pltpu.VMEM)] * 7,
+        in_specs=[pl.BlockSpec(memory_space=pltpu.VMEM)] * 8,
         out_specs=[pl.BlockSpec(memory_space=pltpu.VMEM)] * 5,
         name="own_rows",
         compiler_params=pltpu.CompilerParams(vmem_limit_bytes=VMEM_LIMIT),
-    )(gains, attn_in, mlp_in, proj, gu, down, out)
+    )(attn_gain, mlp_gain, attn_in, mlp_in, proj, gu, down, out)
 
 
 def shards(tokens, positions, attn_in, attn_out, attn_gain, mlp_in, mlp_down, mlp_gain, cotangent):
     rows = tokens.shape[0]
     count = 4 * rows
-    gains = jnp.stack([attn_gain, mlp_gain], 1)
+    attn_gain, mlp_gain = attn_gain[None], mlp_gain[None]
     lanes = np.arange(128)
     freqs = np.zeros((8, 128), np.float32)
     freqs[0] = np.float32(ROPE_BASE) ** (-2.0 * (lanes % 32).astype(np.float32) / HEAD_DIM)
     freqs[1] = np.where(lanes % 64 < 32, -1.0, 1.0)
     (normed_one_all, cot_all, proj_w, gu_w, down_w, out_w, q_all, kv_all, attended_low, lse, cosines, sines, bias_all, middle, two_all) = (
-        forward_attention(tokens, cotangent, positions[None], freqs, gains, attn_in, mlp_in, mlp_down, attn_out, 0)
+        forward_attention(tokens, cotangent, positions[None], freqs, attn_gain, mlp_gain, attn_in, mlp_in, mlp_down, attn_out, 0)
     )
     branch_all, grad_middle, gu_a, gu_b, sum_down, out_part = feed_forward(
         two_all, cot_all, gu_w, down_w, middle, cotangent, 1
@@ -1476,7 +1482,7 @@
         cosines, sines, bias_all, q_all, kv_all.reshape(2 * count, 128), attended_low, lse, normed_one_all, proj_w, out_w, 2,
     )
     grad_in, grad_mlp, grad_down, grad_out, grad_gains = own_rows(
-        gains, attn_in, mlp_in, own_proj, own_gu, own_down, own_out
+        attn_gain, mlp_gain, attn_in, mlp_in, own_proj, own_gu, own_down, own_out
     )
     return outputs, input_grad, grad_in, grad_out, grad_gains[0], grad_mlp, grad_down, grad_gains[1]
 

time: 240 us -> 233 us (0.971)
  Pallas kernels: 233 us -> 228 us
    pallas_call x1, Pallas kernels: 64.2 us -> 59.4 us  [backward_attention(): pl.pallas_call(kernel, out_shape=[o[0] for o in outs], in_specs=in_specs,...]
where the time goes in v3:
time: 233 us
  Pallas kernels  228 us (98%)
  local copies, waits for them, and re-layouts  4.13 us (2%)
    pallas_call x1, Pallas kernels, forward_attention(): pl.pallas_call(kernel, out_shape=[o[0] for o in outs], in_specs=[vmem] *...  96.1 us
    pallas_call x1, Pallas kernels, feed_forward(): pl.pallas_call(kernel, out_shape=[struct((4, rows, D)), struct((rows, D),...  70 us
    pallas_call x1, Pallas kernels, backward_attention(): pl.pallas_call(kernel, out_shape=[o[0] for o in outs], in_specs=in_specs,...  59.4 us

profile of v3, /device:TPU:0, one launch (start us, length us, event | category | flops | bytes accessed | tf_op | source)
XLA Modules:
  0.0 232.9 jit_solution(11088620846064925474)
XLA Ops:
  0.6 96.1 %forward_attention.1 = (bf16[4,128,2048]{2,1,0:T(8,128)(2,1)}, bf16[4,128,2048]{2,1,0:T(8,128)(2,1)}, bf16[4,2,2,128,640]{4,3,2,1,0:T(8,128)(2,1)}, bf16[4,2,2,1...) custom-call(bf16[128,2048]{1,0:T(8,128)(2,1)} %tok_hbm.1, ...), custom_call_target="tpu_custom_call" | custom-call | tf_op jit(solution)/shard_map/forward_attention/pallas_call | solution.py:666
  96.7 70.0 %feed_forward.1 = (bf16[4,128,2048]{2,1,0:T(8,128)(2,1)}, f32[128,2048]{1,0:T(8,128)}, bf16[2,128,1664]{2,1,0:T(8,128)(2,1)}, bf16[4,64,1152]{2,1,0:T(8,128)(2,1...) custom-call(bf16[4,128,2048]{2,1,0:T(8,128)(2,1)} %get-tuple-element.40.two_ref, ...), custom_call_target="tpu_custom_call" | custom-call | tf_op jit(solution)/shard_map/feed_forward/pallas_call | solution.py:1378
  166.7 59.4 %backward_attention.1 = (bf16[128,2048]{1,0:T(8,128)(2,1)}, f32[128,2048]{1,0:T(8,128)}, bf16[4,16,640]{2,1,0:T(8,128)(2,1)}, bf16[4,16,2816]{2,1,0:T(8,128)(2,1...) custom-call(bf16[2,128,1664]{2,1,0:T(8,128)(2,1)} %get-tuple-element.45.gu_a_ref, ...), custom_call_target="tpu_custom_call" | custom-call | tf_op jit(solution)/shard_map/backward_attention/pallas_call | solution.py:1101
  226.1 0.0 copy-start
  226.2 2.6 %own_rows.1 = (f32[16,2560]{1,0:T(8,128)}, f32[16,11264]{1,0:T(8,128)}, f32[16,5632]{1,0:T(8,128)}, f32[16,2048]{1,0:T(8,128)}, f32[8,16]{1,0:T(8,128)}) custom-call(bf16[1,16]{1,0:T(2,128)(2,1)} %bitcast.10, bf16[1,16]{1,0:T(2,128)(2,1)} %bitcast.12, bf16[16,2560]{1,0:T(8,128)(2,1)} %in_ref.3, bf16[16,11264]{1,0:T(8,128)(2,1)} %mlp_ref.3, ...), custom_call_target="tpu_custom_call" | custom-call | tf_op jit(solution)/shard_map/own_rows/pallas_call | solution.py:1456
  228.8 1.3 slice_bitcast_fusion
  230.1 1.9 copy.20
  232.0 0.0 copy-done
  232.0 1.0 copy.21
Async XLA Ops:
  226.1 5.8 %copy-start = (f32[128,2048]{1,0:T(8,128)S(1)}, f32[128,2048]{1,0:T(8,128)}, u32[]{:S(2)}) copy-start(f32[128,2048]{1,0:T(8,128)} %get-tuple-element.83) | copy-start | bytes 3145732

commit v4 on v3

--- a/solution.py
+++ b/solution.py
@@ -350,8 +350,8 @@
 
     def kernel(
         tok_ref, cot_ref, spot_ref, freq_ref, one_ref, two_ref, in_ref, mlp_ref, down_ref, wo,
-        normed_out, cot_all, gp, gg, gd, go, q_out, kv_out, att_out, lse_out, cos_out, sin_out, bias_out, middle_out, two_all,
-        wp, wg, wd, tok, normed, wp_v, wo_v, q_s, kv, vx, bias, att, part, halves, whole, spot_all, own_two, cos_s, sin_s, bias_t, send, recv, local,
+        normed_out, cot_all, gp, gg, gd, go, q_out, kv_out, att_out, lse_out, cos_out, sin_out, bias_out, middle_hbm, two_all,
+        wp, wg, wd, tok, normed, wp_v, wo_v, q_s, kv, vx, bias, att, part, halves, whole, spot_all, own_two, middle_out, cos_s, sin_s, bias_t, send, recv, local,
     ):
         say_hello(ALL_LINES, True)
         at = place()
@@ -625,6 +625,8 @@
             lax.fori_loop(0, rows // 64, mid, 0)
             two_rings[k].start()
         two_own.start()
+        middle_save = near(middle_out, middle_hbm)
+        middle_save.start()
         for ring in two_rings:
             ring.turn()
         g_gu.far()
@@ -634,7 +636,7 @@
             ring.far()
         g_gu.finish()
         g_down.finish()
-        for cp in (cot_own, normed_save, q_save, kv_save, att_save, two_own, bias_save, *turn_saves):
+        for cp in (cot_own, normed_save, q_save, kv_save, att_save, two_own, middle_save, bias_save, *turn_saves):
             cp.wait()
         for group in to_y:
             for cp in group:
@@ -659,7 +661,7 @@
         (struct((count, 128), F32), anywhere),
         (struct((count, 128), F32), anywhere),
         (struct((2 * count, count), F32), anywhere),
-        (struct((rows, D), F32), vmem),
+        (struct((rows, D), F32), anywhere),
         (struct((4, rows, D)), anywhere),
     ]
     copies = 9 + 1 + 3 + 6 * 6 + 1 + 31 * 4
@@ -686,12 +688,13 @@
             pltpu.VMEM((2, rows, D), BF16),
             pltpu.VMEM((4, 8, 128), F32),
             pltpu.VMEM((rows, D), BF16),
+            pltpu.VMEM((rows, D), F32),
             pltpu.VMEM((count, 128), F32),
             pltpu.VMEM((count, 128), F32),
             pltpu.VMEM((2 * count, count), F32),
             pltpu.SemaphoreType.DMA((copies,)),
             pltpu.SemaphoreType.DMA((copies,)),
-            pltpu.SemaphoreType.DMA((20,)),
+            pltpu.SemaphoreType.DMA((22,)),
         ],
         name="forward_attention",
         compiler_params=pltpu.CompilerParams(
@@ -1163,9 +1166,9 @@
 
     def kernel(
         two_ref, cot_ref, wg_ref, wd_ref, mid_hbm, own_cot_hbm,
-        branch_all, gm_ref, gu_a, gu_b, s_down, op_out,
+        branch_all, gm_hbm, gu_a, gu_b, s_down, op_out,
         part, halves, whole, two, gu, cot, hid, gh, turned, t_gu, t_down, rc_gu, rc_down, branch, op,
-        mid_ref, own_cot,
+        mid_ref, own_cot, gm_ref,
         far_a, near_a, far_b, near_b, send, recv, local, weights,
     ):
         partners = [along_y(1), along_y(3), along_x(1), along_x(3), along_z(1), along_z(3), sibling]
@@ -1342,6 +1345,8 @@
             lax.fori_loop(0, rows // 64, back, 0)
             gathers[k].start()
         own.start()
+        save_gm = near(gm_ref, gm_hbm)
+        save_gm.start()
         lax.fori_loop(0, 4, part_out, 0)
         save_op.start()
         for gather in gathers:
@@ -1363,6 +1368,7 @@
         for cp in saves_gu:
             cp.start()
         own.wait()
+        save_gm.wait()
         save_op.wait()
         for cp in saves + saves_gu:
             cp.wait()
@@ -1386,7 +1392,7 @@
             struct((4, rows, D)),
         ],
         in_specs=[anywhere] * 6,
-        out_specs=[anywhere, vmem, anywhere, anywhere, anywhere, anywhere],
+        out_specs=[anywhere] * 6,
         scratch_shapes=[
             pltpu.VMEM((4, rows, D), BF16),
             pltpu.VMEM((2, rows, D // 2), BF16),
@@ -1405,10 +1411,11 @@
             pltpu.VMEM((4, rows, D), BF16),
             pltpu.VMEM((rows, D), F32),
             pltpu.VMEM((rows, D), BF16),
+            pltpu.VMEM((rows, D), F32),
             *line_buffers(2 * HID, SPLITS[1][1]),
             pltpu.SemaphoreType.DMA((copies,)),
             pltpu.SemaphoreType.DMA((copies,)),
-            pltpu.SemaphoreType.DMA((16,)),
+            pltpu.SemaphoreType.DMA((18,)),
             pltpu.SemaphoreType.DMA((tiles_gu + pairs + 1,)),
         ],
         name="feed_forward",

time: 233 us -> 232 us (level)
  no operation moved by 1% of the time
where the time goes in v4:
time: 232 us
  Pallas kernels  227 us (98%)
  local copies, waits for them, and re-layouts  4.13 us (2%)
    pallas_call x1, Pallas kernels, forward_attention(): pl.pallas_call(kernel, out_shape=[o[0] for o in outs], in_specs=[vmem] *...  95.7 us
    pallas_call x1, Pallas kernels, feed_forward(): pl.pallas_call(kernel, out_shape=[struct((4, rows, D)), struct((rows, D),...  69 us
    pallas_call x1, Pallas kernels, backward_attention(): pl.pallas_call(kernel, out_shape=[o[0] for o in outs], in_specs=in_specs,...  59.6 us

profile of v4, /device:TPU:0, one launch (start us, length us, event | category | flops | bytes accessed | tf_op | source)
XLA Modules:
  0.0 231.7 jit_solution(9355074168242262598)
XLA Ops:
  0.6 95.7 %forward_attention.1 = (bf16[4,128,2048]{2,1,0:T(8,128)(2,1)}, bf16[4,128,2048]{2,1,0:T(8,128)(2,1)}, bf16[4,2,2,128,640]{4,3,2,1,0:T(8,128)(2,1)}, bf16[4,2,2,1...) custom-call(bf16[128,2048]{1,0:T(8,128)(2,1)} %tok_hbm.1, ...), custom_call_target="tpu_custom_call" | custom-call | tf_op jit(solution)/shard_map/forward_attention/pallas_call | solution.py:668
  96.3 69.0 %feed_forward.1 = (bf16[4,128,2048]{2,1,0:T(8,128)(2,1)}, f32[128,2048]{1,0:T(8,128)}, bf16[2,128,1664]{2,1,0:T(8,128)(2,1)}, bf16[4,64,1152]{2,1,0:T(8,128)(2,1...) custom-call(bf16[4,128,2048]{2,1,0:T(8,128)(2,1)} %get-tuple-element.40.two_ref, ...), custom_call_target="tpu_custom_call" | custom-call | tf_op jit(solution)/shard_map/feed_forward/pallas_call | solution.py:1384
  165.4 59.6 %backward_attention.1 = (bf16[128,2048]{1,0:T(8,128)(2,1)}, f32[128,2048]{1,0:T(8,128)}, bf16[4,16,640]{2,1,0:T(8,128)(2,1)}, bf16[4,16,2816]{2,1,0:T(8,128)(2,1...) custom-call(bf16[2,128,1664]{2,1,0:T(8,128)(2,1)} %get-tuple-element.45.gu_a_ref, ...), custom_call_target="tpu_custom_call" | custom-call | tf_op jit(solution)/shard_map/backward_attention/pallas_call | solution.py:1104
  225.0 0.0 copy-start
  225.0 2.6 %own_rows.1 = (f32[16,2560]{1,0:T(8,128)}, f32[16,11264]{1,0:T(8,128)}, f32[16,5632]{1,0:T(8,128)}, f32[16,2048]{1,0:T(8,128)}, f32[8,16]{1,0:T(8,128)}) custom-call(bf16[1,16]{1,0:T(2,128)(2,1)} %bitcast.10, bf16[1,16]{1,0:T(2,128)(2,1)} %bitcast.12, bf16[16,2560]{1,0:T(8,128)(2,1)} %in_ref.3, bf16[16,11264]{1,0:T(8,128)(2,1)} %mlp_ref.3, ...), custom_call_target="tpu_custom_call" | custom-call | tf_op jit(solution)/shard_map/own_rows/pallas_call | solution.py:1463
  227.6 1.3 slice_bitcast_fusion
  228.9 1.9 copy.20
  230.8 0.0 copy-done
  230.8 1.0 copy.21
Async XLA Ops:
  225.0 5.8 %copy-start = (f32[128,2048]{1,0:T(8,128)S(1)}, f32[128,2048]{1,0:T(8,128)}, u32[]{:S(2)}) copy-start(f32[128,2048]{1,0:T(8,128)} %get-tuple-element.83) | copy-start | bytes 3145732

commit v5 on v4

--- a/solution.py
+++ b/solution.py
@@ -1426,7 +1426,7 @@
 
 
 def own_rows(attn_gain, mlp_gain, attn_in, mlp_in, proj, gu, down, out):
-    def kernel(one_ref, two_ref, in_ref, mlp_ref, proj_ref, gu_ref, down_ref, out_ref, g_in, g_mlp, g_down, g_out, g_gain):
+    def kernel(one_ref, two_ref, in_ref, mlp_ref, proj_ref, gu_ref, down_ref, out_ref, g_in, g_mlp, g_down, g_out, g_one, g_two):
         gain_one, gain_two = column(one_ref), column(two_ref)
         lane = lax.broadcasted_iota(jnp.int32, (16, 128), 1)
         low = lane < 64
@@ -1457,14 +1457,15 @@
             g_down[:, pl.ds(k * HID, HID)] = down_ref[k].astype(F32)
         g_out[...] = out_ref[...].astype(F32)
         sums = jnp.sum(first, -1, keepdims=True), jnp.sum(second, -1, keepdims=True)
-        g_gain[...] = jnp.transpose(jnp.where(lane == 0, sums[0], sums[1]))[0:8]
-
-    shapes = [(16, attn_in.shape[1]), (16, 2 * FF), (16, FF), (16, D), (8, 16)]
+        turned = jnp.transpose(jnp.where(lane == 0, sums[0], sums[1]))
+        g_one[...], g_two[...] = turned[0:1], turned[1:2]
+
+    shapes = [(16, attn_in.shape[1]), (16, 2 * FF), (16, FF), (16, D), (1, 16), (1, 16)]
     return pl.pallas_call(
         kernel,
         out_shape=[struct(shape, F32) for shape in shapes],
         in_specs=[pl.BlockSpec(memory_space=pltpu.VMEM)] * 8,
-        out_specs=[pl.BlockSpec(memory_space=pltpu.VMEM)] * 5,
+        out_specs=[pl.BlockSpec(memory_space=pltpu.VMEM)] * 6,
         name="own_rows",
         compiler_params=pltpu.CompilerParams(vmem_limit_bytes=VMEM_LIMIT),
     )(attn_gain, mlp_gain, attn_in, mlp_in, proj, gu, down, out)
@@ -1488,10 +1489,10 @@
         gu_a, gu_b, sum_down, out_part, branch_all, grad_middle, middle, tokens,
         cosines, sines, bias_all, q_all, kv_all.reshape(2 * count, 128), attended_low, lse, normed_one_all, proj_w, out_w, 2,
     )
-    grad_in, grad_mlp, grad_down, grad_out, grad_gains = own_rows(
+    grad_in, grad_mlp, grad_down, grad_out, grad_one, grad_two = own_rows(
         attn_gain, mlp_gain, attn_in, mlp_in, own_proj, own_gu, own_down, own_out
     )
-    return outputs, input_grad, grad_in, grad_out, grad_gains[0], grad_mlp, grad_down, grad_gains[1]
+    return outputs, input_grad, grad_in, grad_out, grad_one[0], grad_mlp, grad_down, grad_two[0]
 
 
 def solution(mesh):

time: 232 us -> 231 us (level)
  no operation moved by 1% of the time
where the time goes in v5:
time: 231 us; the launch traced here: 230 us
  Pallas kernels  227 us (98%)
  local copies, waits for them, and re-layouts  2.86 us (1%)
    pallas_call x1, Pallas kernels, forward_attention(): pl.pallas_call(kernel, out_shape=[o[0] for o in outs], in_specs=[vmem] *...  95.7 us
    pallas_call x1, Pallas kernels, feed_forward(): pl.pallas_call(kernel, out_shape=[struct((4, rows, D)), struct((rows, D),...  69 us
    pallas_call x1, Pallas kernels, backward_attention(): pl.pallas_call(kernel, out_shape=[o[0] for o in outs], in_specs=in_specs,...  59.4 us

profile of v5, /device:TPU:0, one launch (start us, length us, event | category | flops | bytes accessed | tf_op | source)
XLA Modules:
  0.0 230.3 jit_solution(16106973517392180429)
XLA Ops:
  0.6 95.7 %forward_attention.1 = (bf16[4,128,2048]{2,1,0:T(8,128)(2,1)}, bf16[4,128,2048]{2,1,0:T(8,128)(2,1)}, bf16[4,2,2,128,640]{4,3,2,1,0:T(8,128)(2,1)}, bf16[4,2,2,1...) custom-call(bf16[128,2048]{1,0:T(8,128)(2,1)} %tok_hbm.1, ...), custom_call_target="tpu_custom_call" | custom-call | tf_op jit(solution)/shard_map/forward_attention/pallas_call | solution.py:668
  96.4 69.0 %feed_forward.1 = (bf16[4,128,2048]{2,1,0:T(8,128)(2,1)}, f32[128,2048]{1,0:T(8,128)}, bf16[2,128,1664]{2,1,0:T(8,128)(2,1)}, bf16[4,64,1152]{2,1,0:T(8,128)(2,1...) custom-call(bf16[4,128,2048]{2,1,0:T(8,128)(2,1)} %get-tuple-element.41.two_ref, ...), custom_call_target="tpu_custom_call" | custom-call | tf_op jit(solution)/shard_map/feed_forward/pallas_call | solution.py:1384
  165.4 59.4 %backward_attention.1 = (bf16[128,2048]{1,0:T(8,128)(2,1)}, f32[128,2048]{1,0:T(8,128)}, bf16[4,16,640]{2,1,0:T(8,128)(2,1)}, bf16[4,16,2816]{2,1,0:T(8,128)(2,1...) custom-call(bf16[2,128,1664]{2,1,0:T(8,128)(2,1)} %get-tuple-element.46.gu_a_ref, ...), custom_call_target="tpu_custom_call" | custom-call | tf_op jit(solution)/shard_map/backward_attention/pallas_call | solution.py:1104
  224.8 0.0 copy-start
  224.8 2.6 %own_rows.1 = (f32[16,2560]{1,0:T(8,128)}, f32[16,11264]{1,0:T(8,128)}, f32[16,5632]{1,0:T(8,128)}, f32[16,2048]{1,0:T(8,128)}, f32[1,16]{1,0:T(1,128)}, /*index=5*/f32[1,16]{1,0:T(1,128)}) custom-call(bf16[1,16]{1,0:T(2,128)(2,1)} %bitcast.8, bf16[1,16]{1,0:T(2,128)(2,1)} %bitcast.10, bf16[16,2560]{1,0:T(8,128)(2,1)} %in_ref.3, bf16[16,11264]{1,0:T(8,128)(2,1)} %mlp_ref.3, ...), custom_call_target="tpu_custom_call" | custom-call | tf_op jit(solution)/shard_map/own_rows/pallas_call | solution.py:1464
  227.4 1.9 copy.20
  229.3 0.0 copy-done
  229.3 1.0 copy.21
Async XLA Ops:
  224.8 4.5 %copy-start = (f32[128,2048]{1,0:T(8,128)S(1)}, f32[128,2048]{1,0:T(8,128)}, u32[]{:S(2)}) copy-start(f32[128,2048]{1,0:T(8,128)} %get-tuple-element.83) | copy-start | bytes 3145732
